TPU v7x, 256 devices: a whole 4x4x8 slice. The times are simulated.
256 devices in a mesh: replica: 16 (over y, x_hi, core), tensor: 8 (over z), fsdp: 2 (over x_lo).
Axes of the slice: x: 4 (x_hi: 2, x_lo: 2; x = x_hi * 2 + x_lo), y: 4, z: 8, core: 2. Of those that a mesh axis runs over, the one named last changes fastest.
Arguments:
- tokens: bfloat16 [32768, 8192], P(('replica', 'fsdp'), 'tensor'), may hold values from -600 to 600
- gain: float32 [8192], P('tensor'), may hold values from 0.1 to 1.9
- kv_weight: bfloat16 [16, 8192, 2048], P('replica', 'tensor', 'fsdp'), may hold values from -0.0625 to 0.0625
- local_params: float32 [16, 768, 8192], P('replica', ('tensor', 'fsdp')), may hold values from -70 to 70
- base_params: float32 [768, 8192], P(('tensor', 'fsdp')), may hold values from -6 to 6
- momentum: float32 [768, 8192], P(('tensor', 'fsdp')), may hold values from -6 to 6
Outputs:
- kv_heads: bfloat16 [32768, 2048], P(('replica', 'fsdp'), 'tensor')
- new_base: float32 [768, 8192], P(('tensor', 'fsdp'))
- new_momentum: float32 [768, 8192], P(('tensor', 'fsdp'))
All inputs are finite; a program needn't handle non-finite values.
Results may differ from a plain program's by a relative error of at most 0.017.
Values may be sent and summed in bfloat16 or wider, within the bound.
A program may use at most 64 MiB of HBM per device.

v0:
```python
import jax
import jax.numpy as jnp
from jax import lax
from jax.sharding import PartitionSpec as P

G = 128


outer_momentum = 0.9
outer_rate = 0.7
norm_eps = 1e-05
scale_eps = 1e-06


def quantize(pseudo_grad, group_size):
    row_count, col_count = pseudo_grad.shape
    blocks = pseudo_grad.reshape(row_count, col_count // group_size, group_size)
    scales = lax.optimization_barrier(
        (jnp.max(jnp.abs(blocks), axis=2) + scale_eps).astype(jnp.bfloat16)
    )
    levels = lax.optimization_barrier(
        (blocks / scales.astype(jnp.float32)[:, :, None]).astype(jnp.bfloat16)
    )
    return (levels, scales)


def body(tokens, gain, kv_weight, local_params, base_params, momentum):
    group_size = G
    features = tokens.astype(jnp.float32)
    squares = lax.psum(jnp.sum(features * features, axis=1), "tensor")
    full_width = features.shape[1] * lax.axis_size("tensor")
    mean_square = squares / full_width
    normed = (features * lax.rsqrt(mean_square + norm_eps)[:, None] * gain[None, :]).astype(
        jnp.bfloat16
    )
    partial_value = jnp.dot(
        normed,
        lax.all_gather(kv_weight[0], "fsdp", axis=1, tiled=True),
        preferred_element_type=jnp.float32,
    )
    kv_heads = lax.psum_scatter(
        partial_value.astype(jnp.bfloat16), "tensor", scatter_dimension=1, tiled=True
    )
    pseudo_grad = base_params - local_params[0]
    levels, scales = quantize(pseudo_grad, group_size)
    replicas = lax.axis_size("replica")
    row_count, col_count = pseudo_grad.shape
    values = (levels.astype(jnp.float32) * scales.astype(jnp.float32)[:, :, None]).reshape(
        row_count, col_count
    )
    average = lax.psum(values.astype(jnp.bfloat16), "replica").astype(jnp.float32) / replicas
    new_momentum = outer_momentum * momentum + average
    new_base = base_params - outer_rate * (average + outer_momentum * new_momentum)
    return (kv_heads, new_base, new_momentum)


def solution(mesh):
    placed = (
        P(("replica", "fsdp"), "tensor"),
        P("tensor"),
        P("replica", "tensor", "fsdp"),
        P("replica", ("tensor", "fsdp"), None),
        P(("tensor", "fsdp"), None),
        P(("tensor", "fsdp"), None),
    )
    return jax.shard_map(
        body,
        mesh=mesh,
        in_specs=placed,
        out_specs=(
            P(("replica", "fsdp"), "tensor"),
            P(("tensor", "fsdp"), None),
            P(("tensor", "fsdp"), None),
        ),
        check_vma=False,
    )
```

profile of v0, /device:TPU:1, one launch (start us, length us, event | category | flops | bytes accessed | tf_op | source)
XLA Modules:
  0.0 215.7 jit_solution(12078905422262266330)
XLA Ops:
  8.0 0.0 copy-start
  8.0 0.0 all-gather.3.cloned.1.call-start
  8.1 0.7 all-gather.3.cloned.1.call-update
  8.7 0.0 all-reduce.2.cloned.1.call-start
  8.8 0.6 copy-done
  9.4 1.6 fusion.11
  11.0 0.3 copy.9
  11.3 0.5 abs_reduce_fusion
  11.8 0.5 divide_convert_fusion
  12.2 0.5 multiply_convert_fusion
  12.7 1.4 copy.12
  14.1 0.0 copy-start.2
  14.1 0.0 all-reduce.2.cloned.1.call-update
  14.2 0.0 reduce-scatter.2.cloned.1.call-start
  14.2 2.1 fusion
  16.3 17.5 %psum.14 = f32[1024]{0:T(1024)S(1)} all-reduce(f32[1024]{0:T(1024)S(1)} %fusion), channel_id=1, replica_groups=mesh['replica'=16,'tensor'=8,'fsdp'=2] {'tensor'}, use_global_device_ids=true, to_apply=%region_1.0 | all-reduce | flops 1024 | bytes 8192 | tf_op jit(solution)/shard_map/psum | solution.py:30
  33.8 43.0 %all-gather.3.cloned.1.call-done = bf16[1,1024,2048]{2,1,0:T(8,128)(2,1)} async-done(((bf16[1,1024,1024]{2,1,0:T(8,128)(2,1)}), bf16[1,1024,2048]{2,1,0:T(8,128)(2,1)}) %all-gather.3.cloned.1.call-update) | async-done | bytes 4194320 | tf_op jit(solution)/shard_map/all_gather | solution.py:38
  76.7 0.0 copy-done.2
  76.7 9.3 %fusion.5 = bf16[1024,2048]{1,0:T(8,128)(2,1)} fusion(bf16[1,1024,2048]{2,1,0:T(8,128)(2,1)} %all-gather.3.cloned.1.call-done, bf16[1024,1024]{1,0:T(8,128)(2,1)} %param.6, f32[1024]{0:T(1024)S(1)} %copy-done.2, f32[1024]{0:T(1024)S(1)} %add_rsqrt_fusion), kind=kOutput, calls=%fused_computation.7 | convolution fusion | flops 4301258752 | bytes 10493952 | tf_op jit(solution)/shard_map/dot_general | solution.py:36
  86.1 0.0 copy-start.1
  86.1 0.0 reduce-scatter.2.cloned.1.call-update
  86.1 119.0 %all-reduce.2.cloned.1.call-done = bf16[48,8192]{1,0:T(8,128)(2,1)} async-done(((bf16[48,8192]{1,0:T(8,128)(2,1)}), bf16[48,8192]{1,0:T(8,128)(2,1)}) %all-reduce.2.cloned.1.call-update) | async-done | bytes 786448 | tf_op jit(solution)/shard_map/psum | solution.py:51
  205.1 0.0 copy-done.1
  205.1 3.2 %multiply_subtract_fusion = (f32[48,8192]{1,0:T(8,128)}, f32[48,8192]{1,0:T(8,128)}) fusion(f32[48,8192]{1,0:T(8,128)S(1)} %copy-done, bf16[48,8192]{1,0:T(8,128)(2,1)} %all-reduce.2.cloned.1.call-done, f32[48,8192]{1,0:T(8,128)S(1)} %copy-done.1), kind=kLoop, calls=%fused_computation.12 | loop fusion | flops 3145728 | bytes 7077888 | tf_op jit(solution)/shard_map/sub | solution.py:53
  (4 shorter events, 0.0 us)
Async XLA Ops:
  8.0 1.4 copy-start
  8.0 68.7 %all-gather.3.cloned.1.call-start = ((), (), s32[]{:S(2)}) async-start(), calls=%async_computation.3 | async-start | bytes 6291456 | tf_op jit(solution)/shard_map/all_gather | solution.py:38
  8.7 196.3 %all-reduce.2.cloned.1.call-start = ((), (), s32[]{:S(2)}) async-start(), calls=%async_computation.2 | async-start | bytes 1572864 | tf_op jit(solution)/shard_map/psum | solution.py:51
  14.1 62.6 %copy-start.2 = (f32[1024]{0:T(1024)S(1)}, f32[1024]{0:T(1024)}, u32[]{:S(2)}) copy-start(f32[1024]{0:T(1024)} %param.7) | copy-start | bytes 12292
  14.2 194.1 %reduce-scatter.2.cloned.1.call-start = ((), (), s32[]{:S(2)}) async-start(), calls=%async_computation.1 | async-start | bytes 4718592 | tf_op jit(solution)/shard_map/reduce_scatter | solution.py:41
  86.1 119.0 %copy-start.1 = (f32[48,8192]{1,0:T(8,128)S(1)}, f32[48,8192]{1,0:T(8,128)}, u32[]{:S(2)}) copy-start(f32[48,8192]{1,0:T(8,128)} %param.11) | copy-start | bytes 4718596
Sparse Core Ops, SparseCore 0:
  10.6 66.0 all-gather.2
  86.2 56.6 reduce-scatter.1
Sparse Core Ops, SparseCore 1:
  14.2 190.8 all-reduce.1
where the time goes:
time: 216 us
  waiting for transfers between devices  163 us (75%)
  blocking collectives  17.5 us (8%)
  between operations  15.5 us (7%)
  matrix products  9.33 us (4%)
  other arithmetic  8.28 us (4%)
  local copies, waits for them, and re-layouts  2.3 us (1%)
    psum x1, waiting for transfers between devices, body(): lax.psum(values.astype(jnp.bfloat16), 'replica').astype(jnp.float32)  119 us
    all_gather x1, waiting for transfers between devices, body(): lax.all_gather(kv_weight[0], 'fsdp', axis=1, tiled=True)  43 us
    psum x1, blocking collectives, body(): squares = lax.psum(jnp.sum(features * features, axis=1), 'tensor')  17.5 us
    dot_general x1, matrix products, body(): jnp.dot(normed, lax.all_gather(kv_weight[0], 'fsdp', axis=1, tiled=True),...  9.33 us
  transfers between devices with their start and end apart: 3, of which 2 were waited for; matrix products, arithmetic and copies ran while one was open for 9% of the time, Pallas kernels for 0%

commit v1 on v0

v1 whole, which is shorter than its diff:
```python
import jax
import jax.numpy as jnp
from jax import lax
from jax.experimental import pallas as pl
from jax.experimental.pallas import tpu as pltpu
from jax.sharding import PartitionSpec as P

F32 = jnp.float32
BF16 = jnp.bfloat16
MESH = pl.DeviceIdType.MESH

G = 128
OUTER_MOMENTUM = 0.9
OUTER_RATE = 0.7
NORM_EPS = 1e-05
SCALE_EPS = 1e-06
REPLICAS = 16
WIDTH = 8192
RING = 8
TOK = 1024
FEAT = 1024
COLS = 48
HALF = TOK // 2
FROWS = 48
FCOLS = 1024

ORDER = (
    (1, 0, 3, 2, 40, 51, 8, 41, 28, 29, 42, 9, 26, 43, 27, 36, 10, 24, 37, 48, 25, 38, 11, 39, 20, 32, 49, 33, 12, 22, 34, 23, 13, 46, 47, 21, 35, 14, 50, 18, 15, 19, 16, 17),
    (0, 1, 3, 2, 51, 8, 46, 47, 36, 9, 28, 29, 37, 38, 10, 18, 24, 39, 48, 19, 32, 11, 26, 33, 27, 49, 34, 12, 25, 35, 16, 40, 13, 17, 41, 42, 14, 22, 23, 43, 50, 15, 20, 21),
    (3, 2, 0, 1, 51, 8, 28, 29, 22, 9, 46, 47, 23, 20, 10, 32, 42, 21, 48, 33, 18, 11, 40, 19, 41, 49, 16, 12, 43, 17, 34, 26, 13, 35, 27, 24, 14, 36, 37, 25, 50, 15, 38, 39),
    (2, 3, 0, 1, 26, 51, 8, 27, 46, 47, 24, 9, 40, 25, 41, 22, 10, 42, 23, 48, 43, 20, 11, 21, 38, 18, 49, 19, 12, 36, 16, 37, 13, 28, 29, 39, 17, 14, 50, 32, 15, 33, 34, 35),
    (1, 3, 0, 2, 28, 46, 29, 47, 8, 51, 40, 26, 27, 41, 9, 24, 42, 25, 43, 10, 22, 36, 48, 23, 37, 11, 20, 38, 49, 16, 39, 12, 17, 34, 21, 13, 32, 18, 33, 19, 14, 35, 50, 15),
    (0, 3, 2, 1, 28, 40, 29, 41, 8, 51, 46, 26, 27, 42, 9, 22, 43, 24, 47, 10, 20, 48, 38, 21, 11, 39, 25, 32, 49, 23, 12, 33, 16, 34, 17, 13, 35, 36, 37, 14, 18, 50, 19, 15),
    (3, 0, 1, 2, 46, 26, 47, 27, 8, 51, 28, 40, 41, 24, 9, 36, 25, 42, 29, 10, 38, 48, 20, 39, 11, 21, 43, 18, 49, 37, 12, 19, 34, 16, 35, 13, 17, 22, 23, 14, 32, 50, 33, 15),
    (2, 0, 3, 1, 46, 28, 47, 29, 8, 51, 26, 40, 41, 27, 9, 42, 24, 43, 25, 10, 36, 22, 48, 37, 23, 11, 38, 20, 49, 34, 21, 12, 35, 16, 39, 13, 18, 32, 19, 33, 14, 17, 50, 15),
)
ARRIVAL = (
    (8, 11, 10, 12, 13, 9, 15, 14),
    (11, 10, 12, 13, 8, 9, 15, 14),
    (12, 13, 11, 10, 15, 14, 8, 9),
    (15, 12, 13, 11, 10, 14, 8, 9),
    (14, 15, 12, 13, 11, 10, 9, 8),
    (15, 8, 12, 9, 13, 14, 11, 10),
    (8, 15, 11, 14, 10, 9, 12, 13),
    (9, 8, 11, 10, 12, 13, 14, 15),
)


def pick(values, place):
    value = jnp.int32(values[0])
    for c in range(1, RING):
        value = jnp.where(place == c, jnp.int32(values[c]), value)
    return value


def packed(codes, bits):
    return sum(code << (bits * i) for i, code in enumerate(codes))


def kernel(
    tokens, gain, weight, local, base, momentum,
    out, out_base, out_mom,
    tok, xg, gvec, wl, wr, prod, sbuf, rbuf, sq, sqr, rsf, outv,
    bv, lv, mv, vbuf, frecv, fsum, xr, fown, fall,
    load_sem, store_sem, xs, xrs, zs, zr, qs, qr, fs, fr, hs, hr, gs, gr,
):
    rep = lax.axis_index("replica")
    t = lax.axis_index("tensor")
    f = lax.axis_index("fsdp")
    place = lax.rem(t + 4 * f, RING)
    other = lax.rem(place + 4, RING)
    y = rep // 4
    xh = lax.rem(rep // 2, 2)
    core = lax.rem(rep, 2)
    k = y * 2 + core

    def member(delta):
        p = lax.rem(k + delta, RING)
        return p, ((p // 2) * 4 + xh * 2 + lax.rem(p, 2), t, f)

    def on_ring(delta):
        return (rep, lax.rem(t + delta, RING), f)

    x_dev = (rep, t, 1 - f)
    h_dev = (y * 4 + (1 - xh) * 2 + core, t, f)

    loads = []
    for i, (src, dst) in enumerate(
        ((tokens, tok), (gain, gvec), (weight.at[0], wl), (base, bv), (local.at[0], lv), (momentum, mv))
    ):
        loads.append(pltpu.make_async_copy(src, dst, load_sem.at[i]))
        loads[-1].start()

    barrier = pltpu.get_barrier_semaphore()
    pl.semaphore_signal(barrier, inc=1, device_id=x_dev, device_id_type=MESH)
    pl.semaphore_signal(barrier, inc=1, device_id=h_dev, device_id_type=MESH)
    for delta in range(1, RING):
        pl.semaphore_signal(barrier, inc=1, device_id=on_ring(delta), device_id_type=MESH)
        pl.semaphore_signal(barrier, inc=1, device_id=member(delta)[1], device_id_type=MESH)
    pl.semaphore_wait(barrier, 2 + 2 * (RING - 1))

    x_copies = []
    for j in range(8):
        part = pick([row[j] - 8 for row in ARRIVAL], other)
        x_copies.append(
            pltpu.make_async_remote_copy(
                src_ref=weight.at[0, :, pl.ds(pl.multiple_of(part * 128, 128), 128)],
                dst_ref=wr.at[j],
                send_sem=xs.at[j],
                recv_sem=xrs.at[j],
                device_id=x_dev,
                device_id_type=MESH,
            )
        )
        x_copies[-1].start()

    words = [
        pick([packed(row[n : n + 5], 6) for row in ORDER], place) for n in range(0, len(ORDER[0]), 5)
    ]
    arrival = pick([packed([u - 8 for u in row], 3) for row in ARRIVAL], place)

    loads[0].wait()
    loads[1].wait()

    @pl.loop(0, TOK // 128)
    def _(i):
        rows = pl.ds(pl.multiple_of(i * 128, 128), 128)
        xg[rows, :] = (tok[rows, :].astype(F32) * gvec[...]).astype(BF16)

    loads[2].wait()

    def sq_copy(delta):
        return pltpu.make_async_remote_copy(
            src_ref=sq, dst_ref=sqr.at[delta - 1], send_sem=qs.at[delta - 1], recv_sem=qr.at[delta - 1],
            device_id=on_ring(delta), device_id_type=MESH,
        )

    def rs_copy(delta):
        p, dev = member(delta)
        return pltpu.make_async_remote_copy(
            src_ref=vbuf.at[p], dst_ref=frecv.at[delta - 1], send_sem=fs.at[delta - 1],
            recv_sem=fr.at[delta - 1], device_id=dev, device_id_type=MESH,
        )

    def h_copy():
        return pltpu.make_async_remote_copy(
            src_ref=fsum, dst_ref=xr, send_sem=hs.at[0], recv_sem=hr.at[0], device_id=h_dev, device_id_type=MESH
        )

    def ag_copy(delta):
        return pltpu.make_async_remote_copy(
            src_ref=fown, dst_ref=fall.at[delta - 1], send_sem=gs.at[delta - 1], recv_sem=gr.at[delta - 1],
            device_id=member(delta)[1], device_id_type=MESH,
        )

    def z_copy(idx, h, dev):
        return pltpu.make_async_remote_copy(
            src_ref=sbuf.at[idx, h], dst_ref=rbuf.at[idx, h], send_sem=zs.at[idx * 2 + h],
            recv_sem=zr.at[idx * 2 + h], device_id=dev, device_id_type=MESH,
        )

    def own_product(q):
        cols = pl.ds(pl.multiple_of(q * 256, 256), 256)

        @pl.loop(0, TOK // 256)
        def _(i):
            rows = pl.ds(pl.multiple_of(i * 256, 256), 256)
            res = jnp.dot(xg[rows, :], wl[:, cols], preferred_element_type=F32)
            part = pl.ds(pl.multiple_of(lax.rem(i, 2) * 256, 256), 256)
            prod[2 * q, i // 2, part, :] = res[:, :128]
            prod[2 * q + 1, i // 2, part, :] = res[:, 128:]

    def other_product(j):
        pltpu.make_async_remote_copy(
            src_ref=wr.at[j], dst_ref=wr.at[j], send_sem=xs.at[j], recv_sem=xrs.at[j],
            device_id=x_dev, device_id_type=MESH,
        ).wait_recv()
        u = 8 + lax.bitwise_and(lax.shift_right_logical(arrival, 3 * j), jnp.int32(7))

        @pl.loop(0, TOK // 256)
        def _(i):
            rows = pl.ds(pl.multiple_of(i * 256, 256), 256)
            part = pl.ds(pl.multiple_of(lax.rem(i, 2) * 256, 256), 256)
            prod[u, i // 2, part, :] = jnp.dot(xg[rows, :], wr[j], preferred_element_type=F32)

    def pass_on(code):
        h = lax.rem(code, 2)
        idx = code // 2
        up = idx // 8
        r = lax.rem(idx, 8) // 2 + 1
        s = lax.rem(idx, 2)
        step = 2 * up - 1
        u = 2 * lax.rem(place + step * r + RING, RING) + s
        dev = on_ring(step + RING)
        first = (r == 4) | ((r == 3) & (s == 1 - up))

        @pl.when(first)
        def _():
            @pl.loop(0, HALF // 128)
            def _(i):
                rows = pl.ds(pl.multiple_of(i * 128, 128), 128)
                sbuf[idx, h, rows, :] = prod[u, h, rows, :].astype(BF16)

        @pl.when(jnp.logical_not(first))
        def _():
            z_copy(idx + 2, h, dev).wait_recv()

            @pl.loop(0, HALF // 128)
            def _(i):
                rows = pl.ds(pl.multiple_of(i * 128, 128), 128)
                sbuf[idx, h, rows, :] = (
                    prod[u, h, rows, :] + rbuf[idx + 2, h, rows, :].astype(F32)
                ).astype(BF16)

        z_copy(idx, h, dev).start()

    def fragment_start():
        ones = jnp.ones((16, FEAT), BF16)
        sub = lax.broadcasted_iota(jnp.int32, (8, 128), 0)
        acc = jnp.zeros((8, 128), F32)
        for i in range(TOK // 256):
            x = tok[i * 256 : (i + 1) * 256, :].astype(F32)
            x2 = x * x
            hi = x2.astype(BF16)
            lo = (x2 - hi.astype(F32)).astype(BF16)
            dims = (((1,), (1,)), ((), ()))
            row = lax.dot_general(ones, hi, dims, preferred_element_type=F32)
            row = row + lax.dot_general(ones, lo, dims, preferred_element_type=F32)
            for g in range(2):
                acc = acc + jnp.where(sub == 2 * i + g, row[0:8, g * 128 : (g + 1) * 128], 0.0)
        sq[...] = acc
        for delta in range(1, RING):
            sq_copy(delta).start()

        loads[3].wait()
        loads[4].wait()

        @pl.loop(0, RING)
        def _(p):
            for g in range(FCOLS // G):
                cols = pl.ds(pl.multiple_of(p * FCOLS + g * G, G), G)
                grad = bv[:, cols] - lv[:, cols]
                top = jnp.max(jnp.abs(grad), axis=1, keepdims=True)
                scale = (top + SCALE_EPS).astype(BF16).astype(F32)
                level = (grad / scale).astype(BF16).astype(F32)
                vbuf[p, :, g * G : (g + 1) * G] = (level * scale).astype(BF16)

        for delta in range(1, RING):
            rs_copy(delta).start()

    def fragment_sum():
        for delta in range(1, RING):
            rs_copy(delta).wait_recv()
        total = vbuf[k].astype(F32)
        for delta in range(1, RING):
            total = total + frecv[delta - 1].astype(F32)
        fsum[...] = total.astype(BF16)
        h_copy().start()

    def fragment_spread():
        h_copy().wait_recv()
        fown[...] = (fsum[...].astype(F32) + xr[...].astype(F32)).astype(BF16)
        for delta in range(1, RING):
            ag_copy(delta).start()

    stores = [
        pltpu.make_async_copy(bv, out_base, store_sem.at[0]),
        pltpu.make_async_copy(mv, out_mom, store_sem.at[1]),
    ]

    def fragment_end():
        for delta in range(1, RING):
            ag_copy(delta).wait_recv()
        loads[5].wait()

        for delta in range(RING):
            p = lax.rem(k + RING - delta, RING)
            cols = pl.ds(pl.multiple_of(p * FCOLS, FCOLS), FCOLS)
            piece = fown[...] if delta == 0 else fall[delta - 1]
            average = piece.astype(F32) / REPLICAS
            new_mom = OUTER_MOMENTUM * mv[:, cols] + average
            mv[:, cols] = new_mom
            bv[:, cols] = bv[:, cols] - OUTER_RATE * (average + OUTER_MOMENTUM * new_mom)

        for store in stores:
            store.start()

        total = sq[...]
        for delta in range(1, RING):
            sq_copy(delta).wait_recv()
            total = total + sqr[delta - 1]
        rs = lax.rsqrt(total / WIDTH + NORM_EPS)
        for g in range(TOK // 128):
            rsf[g // 4, g % 4 * 128 : (g % 4 + 1) * 128, :] = jnp.broadcast_to(rs[g : g + 1, :], (128, 128)).T

    @pl.loop(0, len(ORDER[0]))
    def _(n):
        word = words[0]
        for i in range(1, len(words)):
            word = jnp.where(n // 5 == i, words[i], word)
        code = lax.bitwise_and(lax.shift_right_logical(word, 6 * lax.rem(n, 5)), jnp.int32(63))

        @pl.when(code < 8)
        def _():
            own_product(code)

        @pl.when((code >= 8) & (code < 16))
        def _():
            other_product(code - 8)

        @pl.when((code >= 16) & (code < 48))
        def _():
            pass_on(code - 16)

        @pl.when(code == 51)
        def _():
            fragment_start()

        @pl.when(code == 48)
        def _():
            fragment_sum()

        @pl.when(code == 49)
        def _():
            fragment_spread()

        @pl.when(code == 50)
        def _():
            fragment_end()

    for h in range(2):
        for s in range(2):
            z_copy(s, h, on_ring(1)).wait_recv()
            z_copy(8 + s, h, on_ring(1)).wait_recv()

            @pl.loop(0, HALF // 128)
            def _(i):
                rows = pl.ds(pl.multiple_of(i * 128, 128), 128)
                total = prod[2 * place + s, h, rows, :] + rbuf[s, h, rows, :].astype(F32)
                total = total + rbuf[8 + s, h, rows, :].astype(F32)
                outv[h, rows, s * 128 : (s + 1) * 128] = (total * rsf[h, rows, :]).astype(BF16)

        stores.append(
            pltpu.make_async_copy(
                outv.at[h], out.at[pl.ds(h * HALF, HALF)], store_sem.at[2 + h]
            )
        )
        stores[-1].start()

    for copy in x_copies:
        copy.wait_send()
    for idx in range(16):
        if idx in (6 + 1, 8 + 6):
            continue
        for h in range(2):
            z_copy(idx, h, on_ring(1)).wait_send()
    for delta in range(1, RING):
        sq_copy(delta).wait_send()
        rs_copy(delta).wait_send()
        ag_copy(delta).wait_send()
    h_copy().wait_send()
    for store in stores:
        store.wait()


def body(tokens, gain, weight, local, base, momentum):
    dma = pltpu.SemaphoreType.DMA
    any_spec = pl.BlockSpec(memory_space=pl.ANY)
    return pl.pallas_call(
        kernel,
        out_shape=(
            jax.ShapeDtypeStruct((TOK, 256), BF16),
            jax.ShapeDtypeStruct(base.shape, F32),
            jax.ShapeDtypeStruct(base.shape, F32),
        ),
        in_specs=[any_spec] * 6,
        out_specs=[any_spec] * 3,
        scratch_shapes=[
            pltpu.VMEM((TOK, FEAT), BF16),
            pltpu.VMEM((TOK, FEAT), BF16),
            pltpu.VMEM((1, FEAT), F32),
            pltpu.VMEM((FEAT, 1024), BF16),
            pltpu.VMEM((8, FEAT, 128), BF16),
            pltpu.VMEM((16, 2, HALF, 128), F32),
            pltpu.VMEM((16, 2, HALF, 128), BF16),
            pltpu.VMEM((16, 2, HALF, 128), BF16),
            pltpu.VMEM((8, 128), F32),
            pltpu.VMEM((RING - 1, 8, 128), F32),
            pltpu.VMEM((2, HALF, 128), F32),
            pltpu.VMEM((2, HALF, 256), BF16),
            pltpu.VMEM((FROWS, WIDTH), F32),
            pltpu.VMEM((FROWS, WIDTH), F32),
            pltpu.VMEM((FROWS, WIDTH), F32),
            pltpu.VMEM((RING, FROWS, FCOLS), BF16),
            pltpu.VMEM((RING - 1, FROWS, FCOLS), BF16),
            pltpu.VMEM((FROWS, FCOLS), BF16),
            pltpu.VMEM((FROWS, FCOLS), BF16),
            pltpu.VMEM((FROWS, FCOLS), BF16),
            pltpu.VMEM((RING - 1, FROWS, FCOLS), BF16),
            dma((6,)),
            dma((4,)),
            dma((8,)),
            dma((8,)),
            dma((32,)),
            dma((32,)),
            dma((RING - 1,)),
            dma((RING - 1,)),
            dma((RING - 1,)),
            dma((RING - 1,)),
            dma((1,)),
            dma((1,)),
            dma((RING - 1,)),
            dma((RING - 1,)),
        ],
        compiler_params=pltpu.CompilerParams(
            collective_id=0, has_side_effects=True, vmem_limit_bytes=50 * 1024 * 1024
        ),
    )(tokens, gain.reshape(1, FEAT), weight, local, base, momentum)


def solution(mesh):
    placed = (
        P(("replica", "fsdp"), "tensor"),
        P("tensor"),
        P("replica", "tensor", "fsdp"),
        P("replica", ("tensor", "fsdp"), None),
        P(("tensor", "fsdp"), None),
        P(("tensor", "fsdp"), None),
    )
    return jax.shard_map(
        body,
        mesh=mesh,
        in_specs=placed,
        out_specs=(
            P(("replica", "fsdp"), "tensor"),
            P(("tensor", "fsdp"), None),
            P(("tensor", "fsdp"), None),
        ),
        check_vma=False,
    )
```

time: 216 us -> 93 us (0.43)
  the two profiles are of different devices: /device:TPU:1 before, /device:TPU:2 now
where the time goes in v1:
time: 93 us; the launch traced here: 92.9 us
  Pallas kernels  88.5 us (95%)
  local copies, waits for them, and re-layouts  3.76 us (4%)
    pallas_call x1, Pallas kernels, body(): pl.pallas_call(kernel, out_shape=(jax.ShapeDtypeStruct((TOK, 256), BF16),...  88.5 us
    unnamed x5, local copies, waits for them, and re-layouts  3.76 us

profile of v1, /device:TPU:2, one launch (start us, length us, event | category | flops | bytes accessed | tf_op | source)
XLA Modules:
  0.0 92.9 jit_solution(11610641285117627667)
XLA Ops:
  0.6 0.0 copy-start
  0.6 0.7 copy-done
  1.3 88.5 %shard_map.85 = (bf16[1024,256]{1,0:T(8,128)(2,1)S(1)}, f32[48,8192]{1,0:T(8,128)S(1)}, f32[48,8192]{1,0:T(8,128)S(1)}) custom-call(bf16[1024,1024]{1,0:T(8,128)(2,1)} %tokens.1, f32[1,1024]{1,0:T(1,128)S(1)} %bitcast.1, bf16[1,1024,1024]{2,1,0:T(8,128)(2,1)} %weight.1, f32[1,48,8192]{2,1,0:T(8,128)} %local.1, f32[48,8192]{1,0:T(8,128)} %base.1, ...), custom_call_target="tpu_custom_call" | custom-call | tf_op jit(solution)/shard_map/pallas_call | solution.py:369
  89.8 0.8 copy.12
  90.6 1.1 %copy.13 = f32[48,8192]{1,0:T(8,128)} copy(f32[48,8192]{1,0:T(8,128)S(1)} %get-tuple-element.7) | data formatting | bytes 3145728
  91.8 1.1 %copy.14 = f32[48,8192]{1,0:T(8,128)} copy(f32[48,8192]{1,0:T(8,128)S(1)} %get-tuple-element.8) | data formatting | bytes 3145728
Async XLA Ops:
  0.6 0.7 copy-start

commit v2 on v1

--- a/solution.py
+++ b/solution.py
@@ -20,29 +20,78 @@
 TOK = 1024
 FEAT = 1024
 COLS = 48
-HALF = TOK // 2
+CUT = 4
+PART = TOK // CUT
 FROWS = 48
 FCOLS = 1024
 
 ORDER = (
-    (1, 0, 3, 2, 40, 51, 8, 41, 28, 29, 42, 9, 26, 43, 27, 36, 10, 24, 37, 48, 25, 38, 11, 39, 20, 32, 49, 33, 12, 22, 34, 23, 13, 46, 47, 21, 35, 14, 50, 18, 15, 19, 16, 17),
-    (0, 1, 3, 2, 51, 8, 46, 47, 36, 9, 28, 29, 37, 38, 10, 18, 24, 39, 48, 19, 32, 11, 26, 33, 27, 49, 34, 12, 25, 35, 16, 40, 13, 17, 41, 42, 14, 22, 23, 43, 50, 15, 20, 21),
-    (3, 2, 0, 1, 51, 8, 28, 29, 22, 9, 46, 47, 23, 20, 10, 32, 42, 21, 48, 33, 18, 11, 40, 19, 41, 49, 16, 12, 43, 17, 34, 26, 13, 35, 27, 24, 14, 36, 37, 25, 50, 15, 38, 39),
-    (2, 3, 0, 1, 26, 51, 8, 27, 46, 47, 24, 9, 40, 25, 41, 22, 10, 42, 23, 48, 43, 20, 11, 21, 38, 18, 49, 19, 12, 36, 16, 37, 13, 28, 29, 39, 17, 14, 50, 32, 15, 33, 34, 35),
-    (1, 3, 0, 2, 28, 46, 29, 47, 8, 51, 40, 26, 27, 41, 9, 24, 42, 25, 43, 10, 22, 36, 48, 23, 37, 11, 20, 38, 49, 16, 39, 12, 17, 34, 21, 13, 32, 18, 33, 19, 14, 35, 50, 15),
-    (0, 3, 2, 1, 28, 40, 29, 41, 8, 51, 46, 26, 27, 42, 9, 22, 43, 24, 47, 10, 20, 48, 38, 21, 11, 39, 25, 32, 49, 23, 12, 33, 16, 34, 17, 13, 35, 36, 37, 14, 18, 50, 19, 15),
-    (3, 0, 1, 2, 46, 26, 47, 27, 8, 51, 28, 40, 41, 24, 9, 36, 25, 42, 29, 10, 38, 48, 20, 39, 11, 21, 43, 18, 49, 37, 12, 19, 34, 16, 35, 13, 17, 22, 23, 14, 32, 50, 33, 15),
-    (2, 0, 3, 1, 46, 28, 47, 29, 8, 51, 26, 40, 41, 27, 9, 42, 24, 43, 25, 10, 36, 22, 48, 37, 23, 11, 38, 20, 49, 34, 21, 12, 35, 16, 39, 13, 18, 32, 19, 33, 14, 17, 50, 15),
+    (
+        2, 1, 0, 3, 8, 64, 65, 4, 66, 40, 41, 67, 42, 68, 9, 69, 43, 56, 57, 32, 5, 70, 33, 10,
+        71, 36, 34, 60, 37, 61, 35, 58, 38, 11, 52, 39, 59, 53, 24, 62, 6, 25, 54, 26, 55, 27, 12, 63,
+        48, 28, 49, 13, 76, 77, 29, 30, 78, 31, 79, 7, 14, 20, 21, 50, 22, 23, 51, 15, 16, 17, 18, 19,
+    ),
+    (
+        2, 0, 3, 1, 8, 76, 77, 4, 78, 79, 56, 9, 57, 40, 41, 58, 42, 59, 43, 5, 20, 60, 10, 21,
+        61, 48, 22, 49, 23, 62, 32, 11, 63, 33, 52, 34, 53, 35, 50, 16, 6, 64, 17, 51, 18, 12, 36, 54,
+        65, 37, 66, 38, 67, 39, 13, 28, 55, 29, 30, 31, 7, 14, 68, 69, 19, 70, 71, 15, 24, 25, 26, 27,
+    ),
+    (
+        1, 3, 0, 2, 8, 40, 41, 4, 42, 43, 28, 9, 29, 76, 77, 30, 78, 31, 79, 5, 48, 24, 10, 49,
+        25, 20, 50, 21, 51, 26, 68, 11, 27, 69, 16, 70, 17, 71, 22, 52, 6, 36, 53, 23, 54, 12, 64, 18,
+        37, 65, 38, 66, 39, 67, 13, 56, 19, 57, 58, 59, 7, 14, 32, 33, 55, 34, 35, 15, 60, 61, 62, 63,
+    ),
+    (
+        1, 2, 3, 0, 8, 36, 37, 4, 38, 76, 77, 39, 78, 32, 9, 33, 79, 28, 29, 68, 5, 34, 69, 10,
+        35, 64, 70, 24, 65, 25, 71, 30, 66, 11, 16, 67, 31, 17, 60, 26, 6, 61, 18, 62, 19, 63, 12, 27,
+        20, 56, 21, 13, 40, 41, 57, 58, 42, 59, 43, 7, 14, 48, 49, 22, 50, 51, 23, 15, 52, 53, 54, 55,
+    ),
+    (
+        3, 0, 40, 41, 2, 42, 1, 8, 43, 64, 65, 36, 4, 66, 37, 67, 32, 9, 33, 76, 77, 34, 78, 35,
+        79, 38, 5, 10, 39, 60, 24, 61, 25, 56, 20, 62, 11, 68, 69, 26, 27, 70, 71, 6, 21, 57, 22, 58,
+        23, 59, 12, 28, 52, 29, 53, 16, 54, 30, 55, 13, 17, 63, 18, 48, 19, 49, 7, 14, 50, 51, 31, 15,
+    ),
+    (
+        3, 1, 2, 0, 8, 40, 41, 76, 77, 4, 42, 78, 43, 79, 32, 64, 9, 33, 56, 34, 57, 35, 58, 5,
+        59, 28, 10, 20, 65, 21, 66, 22, 67, 23, 52, 11, 29, 53, 30, 68, 31, 54, 36, 6, 69, 37, 70, 24,
+        71, 12, 38, 60, 25, 61, 26, 62, 27, 63, 13, 39, 48, 49, 50, 7, 14, 55, 16, 17, 51, 18, 19, 15,
+    ),
+    (
+        0, 2, 1, 3, 8, 76, 77, 40, 41, 4, 78, 42, 79, 43, 68, 36, 9, 69, 28, 70, 29, 71, 30, 5,
+        31, 56, 10, 48, 37, 49, 38, 50, 39, 51, 16, 11, 57, 17, 58, 32, 59, 18, 64, 6, 33, 65, 34, 60,
+        35, 12, 66, 24, 61, 25, 62, 26, 63, 27, 13, 67, 20, 21, 22, 7, 14, 19, 52, 53, 23, 54, 55, 15,
+    ),
+    (
+        0, 3, 76, 77, 1, 78, 2, 8, 79, 36, 37, 64, 4, 38, 65, 39, 68, 9, 69, 40, 41, 70, 42, 71,
+        43, 66, 5, 10, 67, 24, 60, 25, 61, 28, 48, 26, 11, 32, 33, 62, 63, 34, 35, 6, 49, 29, 50, 30,
+        51, 31, 12, 56, 16, 57, 17, 52, 18, 58, 19, 13, 53, 27, 54, 20, 55, 21, 7, 14, 22, 23, 59, 15,
+    ),
 )
 ARRIVAL = (
-    (8, 11, 10, 12, 13, 9, 15, 14),
-    (11, 10, 12, 13, 8, 9, 15, 14),
-    (12, 13, 11, 10, 15, 14, 8, 9),
-    (15, 12, 13, 11, 10, 14, 8, 9),
-    (14, 15, 12, 13, 11, 10, 9, 8),
-    (15, 8, 12, 9, 13, 14, 11, 10),
-    (8, 15, 11, 14, 10, 9, 12, 13),
-    (9, 8, 11, 10, 12, 13, 14, 15),
+    (
+        8, 10, 11, 12, 13, 9, 15, 14,
+    ),
+    (
+        11, 10, 12, 8, 13, 15, 9, 14,
+    ),
+    (
+        12, 13, 11, 15, 10, 8, 14, 9,
+    ),
+    (
+        15, 13, 12, 11, 10, 14, 8, 9,
+    ),
+    (
+        14, 13, 12, 15, 11, 10, 9, 8,
+    ),
+    (
+        9, 14, 13, 12, 15, 11, 8, 10,
+    ),
+    (
+        14, 9, 10, 11, 8, 12, 15, 13,
+    ),
+    (
+        9, 10, 11, 8, 12, 13, 14, 15,
+    ),
 )
 
 
@@ -112,22 +161,8 @@
                 device_id_type=MESH,
             )
         )
-        x_copies[-1].start()
-
-    words = [
-        pick([packed(row[n : n + 5], 6) for row in ORDER], place) for n in range(0, len(ORDER[0]), 5)
-    ]
-    arrival = pick([packed([u - 8 for u in row], 3) for row in ARRIVAL], place)
-
-    loads[0].wait()
-    loads[1].wait()
-
-    @pl.loop(0, TOK // 128)
-    def _(i):
-        rows = pl.ds(pl.multiple_of(i * 128, 128), 128)
-        xg[rows, :] = (tok[rows, :].astype(F32) * gvec[...]).astype(BF16)
-
-    loads[2].wait()
+    for copy in x_copies[:4]:
+        copy.start()
 
     def sq_copy(delta):
         return pltpu.make_async_remote_copy(
@@ -155,20 +190,47 @@
 
     def z_copy(idx, h, dev):
         return pltpu.make_async_remote_copy(
-            src_ref=sbuf.at[idx, h], dst_ref=rbuf.at[idx, h], send_sem=zs.at[idx * 2 + h],
-            recv_sem=zr.at[idx * 2 + h], device_id=dev, device_id_type=MESH,
-        )
+            src_ref=sbuf.at[idx, h], dst_ref=rbuf.at[idx, h], send_sem=zs.at[idx * CUT + h],
+            recv_sem=zr.at[idx * CUT + h], device_id=dev, device_id_type=MESH,
+        )
+
+    loads[3].wait()
+    loads[4].wait()
+
+    @pl.loop(0, RING)
+    def _(p):
+        for g in range(FCOLS // G):
+            cols = pl.ds(pl.multiple_of(p * FCOLS + g * G, G), G)
+            grad = bv[:, cols] - lv[:, cols]
+            top = jnp.max(jnp.abs(grad), axis=1, keepdims=True)
+            scale = (top + SCALE_EPS).astype(BF16).astype(F32)
+            level = (grad / scale).astype(BF16).astype(F32)
+            vbuf[p, :, g * G : (g + 1) * G] = (level * scale).astype(BF16)
+
+    for delta in range(1, RING):
+        rs_copy(delta).start()
+
+    words = [
+        pick([packed(row[n : n + 4], 7) for row in ORDER], place) for n in range(0, len(ORDER[0]), 4)
+    ]
+    arrival = pick([packed([u - 8 for u in row], 3) for row in ARRIVAL], place)
+
+    loads[0].wait()
+    loads[1].wait()
+
+    @pl.loop(0, TOK // 128)
+    def _(i):
+        rows = pl.ds(pl.multiple_of(i * 128, 128), 128)
+        xg[rows, :] = (tok[rows, :].astype(F32) * gvec[...]).astype(BF16)
+
+    loads[2].wait()
 
     def own_product(q):
         cols = pl.ds(pl.multiple_of(q * 256, 256), 256)
 
-        @pl.loop(0, TOK // 256)
-        def _(i):
-            rows = pl.ds(pl.multiple_of(i * 256, 256), 256)
-            res = jnp.dot(xg[rows, :], wl[:, cols], preferred_element_type=F32)
-            part = pl.ds(pl.multiple_of(lax.rem(i, 2) * 256, 256), 256)
-            prod[2 * q, i // 2, part, :] = res[:, :128]
-            prod[2 * q + 1, i // 2, part, :] = res[:, 128:]
+        res = jnp.dot(xg[...], wl[:, cols], preferred_element_type=F32)
+        prod[2 * q] = res[:, :128].reshape(CUT, PART, 128)
+        prod[2 * q + 1] = res[:, 128:].reshape(CUT, PART, 128)
 
     def other_product(j):
         pltpu.make_async_remote_copy(
@@ -177,15 +239,11 @@
         ).wait_recv()
         u = 8 + lax.bitwise_and(lax.shift_right_logical(arrival, 3 * j), jnp.int32(7))
 
-        @pl.loop(0, TOK // 256)
-        def _(i):
-            rows = pl.ds(pl.multiple_of(i * 256, 256), 256)
-            part = pl.ds(pl.multiple_of(lax.rem(i, 2) * 256, 256), 256)
-            prod[u, i // 2, part, :] = jnp.dot(xg[rows, :], wr[j], preferred_element_type=F32)
+        prod[u] = jnp.dot(xg[...], wr[j], preferred_element_type=F32).reshape(CUT, PART, 128)
 
     def pass_on(code):
-        h = lax.rem(code, 2)
-        idx = code // 2
+        h = lax.rem(code, CUT)
+        idx = code // CUT
         up = idx // 8
         r = lax.rem(idx, 8) // 2 + 1
         s = lax.rem(idx, 2)
@@ -196,7 +254,7 @@
 
         @pl.when(first)
         def _():
-            @pl.loop(0, HALF // 128)
+            @pl.loop(0, PART // 128)
             def _(i):
                 rows = pl.ds(pl.multiple_of(i * 128, 128), 128)
                 sbuf[idx, h, rows, :] = prod[u, h, rows, :].astype(BF16)
@@ -205,7 +263,7 @@
         def _():
             z_copy(idx + 2, h, dev).wait_recv()
 
-            @pl.loop(0, HALF // 128)
+            @pl.loop(0, PART // 128)
             def _(i):
                 rows = pl.ds(pl.multiple_of(i * 128, 128), 128)
                 sbuf[idx, h, rows, :] = (
@@ -214,7 +272,7 @@
 
         z_copy(idx, h, dev).start()
 
-    def fragment_start():
+    def squares():
         ones = jnp.ones((16, FEAT), BF16)
         sub = lax.broadcasted_iota(jnp.int32, (8, 128), 0)
         acc = jnp.zeros((8, 128), F32)
@@ -232,22 +290,6 @@
         for delta in range(1, RING):
             sq_copy(delta).start()
 
-        loads[3].wait()
-        loads[4].wait()
-
-        @pl.loop(0, RING)
-        def _(p):
-            for g in range(FCOLS // G):
-                cols = pl.ds(pl.multiple_of(p * FCOLS + g * G, G), G)
-                grad = bv[:, cols] - lv[:, cols]
-                top = jnp.max(jnp.abs(grad), axis=1, keepdims=True)
-                scale = (top + SCALE_EPS).astype(BF16).astype(F32)
-                level = (grad / scale).astype(BF16).astype(F32)
-                vbuf[p, :, g * G : (g + 1) * G] = (level * scale).astype(BF16)
-
-        for delta in range(1, RING):
-            rs_copy(delta).start()
-
     def fragment_sum():
         for delta in range(1, RING):
             rs_copy(delta).wait_recv()
@@ -256,6 +298,8 @@
             total = total + frecv[delta - 1].astype(F32)
         fsum[...] = total.astype(BF16)
         h_copy().start()
+        for copy in x_copies[4:]:
+            copy.start()
 
     def fragment_spread():
         h_copy().wait_recv()
@@ -291,16 +335,16 @@
             total = total + sqr[delta - 1]
         rs = lax.rsqrt(total / WIDTH + NORM_EPS)
         for g in range(TOK // 128):
-            rsf[g // 4, g % 4 * 128 : (g % 4 + 1) * 128, :] = jnp.broadcast_to(rs[g : g + 1, :], (128, 128)).T
+            rsf[g * 128 // PART, g * 128 % PART : g * 128 % PART + 128, :] = jnp.broadcast_to(rs[g : g + 1, :], (128, 128)).T
 
     @pl.loop(0, len(ORDER[0]))
     def _(n):
         word = words[0]
         for i in range(1, len(words)):
-            word = jnp.where(n // 5 == i, words[i], word)
-        code = lax.bitwise_and(lax.shift_right_logical(word, 6 * lax.rem(n, 5)), jnp.int32(63))
-
-        @pl.when(code < 8)
+            word = jnp.where(n // 4 == i, words[i], word)
+        code = lax.bitwise_and(lax.shift_right_logical(word, 7 * lax.rem(n, 4)), jnp.int32(127))
+
+        @pl.when(code < 4)
         def _():
             own_product(code)
 
@@ -308,32 +352,32 @@
         def _():
             other_product(code - 8)
 
-        @pl.when((code >= 16) & (code < 48))
+        @pl.when(code >= 16)
         def _():
             pass_on(code - 16)
 
-        @pl.when(code == 51)
-        def _():
-            fragment_start()
-
-        @pl.when(code == 48)
+        @pl.when(code == 4)
+        def _():
+            squares()
+
+        @pl.when(code == 5)
         def _():
             fragment_sum()
 
-        @pl.when(code == 49)
+        @pl.when(code == 6)
         def _():
             fragment_spread()
 
-        @pl.when(code == 50)
+        @pl.when(code == 7)
         def _():
             fragment_end()
 
-    for h in range(2):
+    for h in range(CUT):
         for s in range(2):
             z_copy(s, h, on_ring(1)).wait_recv()
             z_copy(8 + s, h, on_ring(1)).wait_recv()
 
-            @pl.loop(0, HALF // 128)
+            @pl.loop(0, PART // 128)
             def _(i):
                 rows = pl.ds(pl.multiple_of(i * 128, 128), 128)
                 total = prod[2 * place + s, h, rows, :] + rbuf[s, h, rows, :].astype(F32)
@@ -342,7 +386,7 @@
 
         stores.append(
             pltpu.make_async_copy(
-                outv.at[h], out.at[pl.ds(h * HALF, HALF)], store_sem.at[2 + h]
+                outv.at[h], out.at[pl.ds(h * PART, PART)], store_sem.at[2 + h]
             )
         )
         stores[-1].start()
@@ -352,7 +396,7 @@
     for idx in range(16):
         if idx in (6 + 1, 8 + 6):
             continue
-        for h in range(2):
+        for h in range(CUT):
             z_copy(idx, h, on_ring(1)).wait_send()
     for delta in range(1, RING):
         sq_copy(delta).wait_send()
@@ -381,13 +425,13 @@
             pltpu.VMEM((1, FEAT), F32),
             pltpu.VMEM((FEAT, 1024), BF16),
             pltpu.VMEM((8, FEAT, 128), BF16),
-            pltpu.VMEM((16, 2, HALF, 128), F32),
-            pltpu.VMEM((16, 2, HALF, 128), BF16),
-            pltpu.VMEM((16, 2, HALF, 128), BF16),
+            pltpu.VMEM((16, CUT, PART, 128), F32),
+            pltpu.VMEM((16, CUT, PART, 128), BF16),
+            pltpu.VMEM((16, CUT, PART, 128), BF16),
             pltpu.VMEM((8, 128), F32),
             pltpu.VMEM((RING - 1, 8, 128), F32),
-            pltpu.VMEM((2, HALF, 128), F32),
-            pltpu.VMEM((2, HALF, 256), BF16),
+            pltpu.VMEM((CUT, PART, 128), F32),
+            pltpu.VMEM((CUT, PART, 256), BF16),
             pltpu.VMEM((FROWS, WIDTH), F32),
             pltpu.VMEM((FROWS, WIDTH), F32),
             pltpu.VMEM((FROWS, WIDTH), F32),
@@ -398,11 +442,11 @@
             pltpu.VMEM((FROWS, FCOLS), BF16),
             pltpu.VMEM((RING - 1, FROWS, FCOLS), BF16),
             dma((6,)),
-            dma((4,)),
+            dma((2 + CUT,)),
             dma((8,)),
             dma((8,)),
-            dma((32,)),
-            dma((32,)),
+            dma((16 * CUT,)),
+            dma((16 * CUT,)),
             dma((RING - 1,)),
             dma((RING - 1,)),
             dma((RING - 1,)),

time: 93 us -> 75.8 us (0.82)
  the two profiles are of different devices: /device:TPU:2 before, /device:TPU:6 now
where the time goes in v2:
time: 75.8 us; the launch traced here: 75.7 us
  Pallas kernels  71.3 us (94%)
  local copies, waits for them, and re-layouts  3.76 us (5%)
    pallas_call x1, Pallas kernels, body(): pl.pallas_call(kernel, out_shape=(jax.ShapeDtypeStruct((TOK, 256), BF16),...  71.3 us
    unnamed x5, local copies, waits for them, and re-layouts  3.76 us

profile of v2, /device:TPU:6, one launch (start us, length us, event | category | flops | bytes accessed | tf_op | source)
XLA Modules:
  0.0 75.7 jit_solution(4640543774747112934)
XLA Ops:
  0.6 0.0 copy-start
  0.6 0.7 copy-done
  1.3 71.3 %shard_map.85 = (bf16[1024,256]{1,0:T(8,128)(2,1)S(1)}, f32[48,8192]{1,0:T(8,128)S(1)}, f32[48,8192]{1,0:T(8,128)S(1)}) custom-call(bf16[1024,1024]{1,0:T(8,128)(2,1)} %tokens.1, f32[1,1024]{1,0:T(1,128)S(1)} %bitcast.1, bf16[1,1024,1024]{2,1,0:T(8,128)(2,1)} %weight.1, f32[1,48,8192]{2,1,0:T(8,128)} %local.1, f32[48,8192]{1,0:T(8,128)} %base.1, ...), custom_call_target="tpu_custom_call" | custom-call | tf_op jit(solution)/shard_map/pallas_call | solution.py:413
  72.6 0.8 %copy.12 = bf16[1024,256]{1,0:T(8,128)(2,1)} copy(bf16[1024,256]{1,0:T(8,128)(2,1)S(1)} %get-tuple-element.6) | data formatting | bytes 1048576
  73.4 1.1 %copy.13 = f32[48,8192]{1,0:T(8,128)} copy(f32[48,8192]{1,0:T(8,128)S(1)} %get-tuple-element.7) | data formatting | bytes 3145728
  74.5 1.1 %copy.14 = f32[48,8192]{1,0:T(8,128)} copy(f32[48,8192]{1,0:T(8,128)S(1)} %get-tuple-element.8) | data formatting | bytes 3145728
Async XLA Ops:
  0.6 0.7 copy-start

commit v3 on v2

v3 whole, which is shorter than its diff:
```python
import jax
import jax.numpy as jnp
from jax import lax
from jax.experimental import pallas as pl
from jax.experimental.pallas import tpu as pltpu
from jax.sharding import PartitionSpec as P

F32 = jnp.float32
BF16 = jnp.bfloat16
MESH = pl.DeviceIdType.MESH

G = 128
OUTER_MOMENTUM = 0.9
OUTER_RATE = 0.7
NORM_EPS = 1e-05
SCALE_EPS = 1e-06
REPLICAS = 16
WIDTH = 8192
RING = 8
FIRST = 5
TOK = 1024
FEAT = 1024
COLS = 48
CUT = 4
PART = TOK // CUT
FROWS = 48
FCOLS = 1024

ORDER = (
    (
        8, 0, 3, 2, 1, 36, 37, 64, 65, 9, 40, 66, 4, 41, 67, 42, 43, 68, 10, 76, 77, 38, 39, 78,
        5, 79, 56, 11, 57, 58, 59, 69, 20, 12, 32, 33, 70, 71, 34, 48, 35, 6, 49, 60, 13, 61, 24, 25,
        62, 21, 80, 63, 26, 50, 7, 14, 51, 27, 22, 52, 53, 23, 54, 15, 28, 55, 29, 30, 31, 16, 17, 18,
        19,
    ),
    (
        2, 1, 0, 8, 76, 77, 3, 78, 4, 79, 9, 40, 41, 56, 42, 57, 43, 58, 10, 59, 20, 60, 21, 68,
        5, 22, 69, 16, 11, 70, 28, 71, 23, 48, 17, 49, 18, 50, 12, 19, 32, 51, 33, 61, 29, 62, 6, 34,
        63, 30, 31, 13, 64, 65, 35, 66, 80, 67, 7, 14, 36, 37, 52, 53, 38, 54, 39, 55, 15, 24, 25, 26,
        27,
    ),
    (
        2, 0, 1, 8, 3, 40, 41, 4, 42, 43, 9, 76, 77, 28, 78, 29, 79, 30, 48, 10, 49, 24, 36, 50,
        31, 51, 5, 25, 52, 26, 11, 68, 27, 69, 37, 70, 20, 71, 38, 12, 64, 39, 65, 21, 66, 22, 6, 67,
        23, 53, 16, 54, 13, 55, 17, 18, 60, 80, 19, 61, 62, 7, 14, 32, 33, 63, 34, 35, 15, 56, 57, 58,
        59,
    ),
    (
        0, 1, 3, 8, 2, 64, 65, 36, 37, 4, 66, 38, 67, 9, 32, 39, 33, 34, 35, 10, 76, 77, 20, 78,
        28, 5, 79, 21, 22, 11, 68, 69, 23, 70, 29, 71, 30, 60, 31, 12, 61, 24, 62, 25, 63, 26, 6, 56,
        27, 57, 16, 58, 13, 59, 40, 41, 42, 80, 43, 7, 14, 17, 52, 18, 53, 54, 19, 55, 15, 48, 49, 50,
        51,
    ),
    (
        3, 2, 0, 8, 40, 41, 1, 42, 76, 77, 4, 43, 56, 9, 28, 57, 36, 58, 29, 59, 30, 78, 31, 10,
        79, 37, 38, 68, 5, 39, 69, 70, 32, 11, 71, 33, 34, 60, 35, 61, 24, 62, 12, 20, 63, 21, 22, 23,
        13, 64, 65, 25, 66, 16, 67, 26, 27, 14, 48, 49, 17, 18, 50, 19, 51, 15, 52, 53, 54, 55, 6, 80,
        7,
    ),
    (
        2, 0, 3, 8, 1, 36, 37, 64, 65, 4, 38, 66, 39, 9, 68, 40, 67, 41, 69, 42, 76, 43, 77, 10,
        24, 78, 25, 79, 5, 26, 70, 32, 71, 11, 28, 29, 30, 31, 12, 48, 49, 27, 33, 50, 34, 51, 35, 52,
        13, 53, 16, 17, 54, 18, 55, 19, 56, 14, 57, 58, 59, 60, 15, 61, 20, 21, 62, 22, 63, 23, 6, 80,
        7,
    ),
    (
        3, 1, 0, 8, 2, 76, 77, 36, 37, 4, 78, 38, 79, 9, 39, 56, 32, 57, 33, 58, 34, 64, 40, 10,
        59, 28, 65, 29, 5, 68, 30, 69, 31, 11, 70, 35, 71, 41, 66, 42, 67, 43, 12, 60, 24, 61, 25, 62,
        26, 63, 27, 13, 20, 21, 14, 22, 23, 48, 49, 15, 16, 50, 17, 18, 51, 19, 52, 6, 53, 54, 55, 80,
        7,
    ),
    (
        3, 0, 1, 8, 2, 76, 77, 40, 41, 4, 78, 42, 79, 9, 36, 64, 37, 65, 38, 66, 39, 67, 43, 10,
        48, 32, 49, 33, 5, 50, 34, 56, 35, 11, 51, 57, 68, 69, 12, 70, 24, 25, 71, 26, 58, 27, 59, 13,
        28, 29, 60, 61, 30, 62, 31, 63, 16, 14, 17, 52, 53, 18, 54, 19, 55, 15, 20, 21, 6, 22, 23, 80,
        7,
    ),
    (
        1, 3, 0, 8, 2, 36, 37, 64, 65, 4, 38, 66, 39, 9, 67, 32, 56, 33, 57, 34, 58, 35, 48, 10,
        49, 50, 5, 52, 28, 53, 11, 29, 76, 30, 77, 31, 78, 79, 12, 40, 41, 60, 42, 61, 43, 62, 63, 13,
        54, 55, 59, 24, 25, 14, 51, 26, 27, 68, 16, 17, 15, 69, 18, 70, 19, 71, 20, 6, 21, 22, 23, 80,
        7,
    ),
    (
        3, 1, 2, 8, 40, 41, 0, 42, 4, 43, 9, 76, 77, 78, 79, 20, 56, 21, 10, 36, 37, 48, 49, 38,
        50, 5, 39, 57, 22, 11, 23, 58, 59, 16, 17, 18, 12, 64, 65, 19, 66, 67, 68, 13, 32, 33, 69, 70,
        34, 71, 35, 52, 14, 24, 25, 53, 54, 26, 51, 27, 55, 15, 28, 29, 60, 30, 31, 61, 6, 62, 63, 80,
        7,
    ),
    (
        0, 2, 3, 8, 1, 76, 77, 4, 78, 79, 9, 28, 29, 30, 68, 31, 69, 10, 24, 40, 70, 25, 71, 5,
        26, 48, 27, 11, 64, 65, 41, 42, 66, 43, 67, 49, 16, 12, 50, 17, 51, 18, 20, 56, 57, 13, 32, 33,
        58, 34, 59, 35, 14, 36, 37, 38, 19, 39, 15, 60, 61, 21, 22, 62, 23, 63, 6, 52, 53, 54, 55, 80,
        7,
    ),
    (
        2, 3, 0, 8, 1, 36, 37, 76, 77, 4, 38, 78, 39, 9, 79, 32, 68, 33, 69, 34, 70, 35, 71, 10,
        20, 64, 21, 65, 5, 22, 66, 23, 67, 11, 24, 60, 25, 61, 26, 62, 28, 63, 12, 40, 41, 42, 43, 13,
        56, 57, 16, 17, 58, 27, 59, 18, 14, 48, 49, 29, 30, 50, 31, 51, 19, 15, 52, 6, 53, 54, 55, 80,
        7,
    ),
    (
        8, 0, 40, 41, 1, 42, 2, 3, 43, 9, 76, 77, 36, 4, 28, 78, 37, 79, 29, 10, 30, 64, 65, 31,
        66, 38, 5, 67, 39, 60, 11, 61, 32, 33, 68, 34, 62, 16, 63, 17, 12, 69, 18, 70, 19, 71, 35, 6,
        52, 24, 53, 25, 54, 13, 20, 56, 26, 57, 80, 21, 58, 22, 7, 14, 59, 48, 23, 27, 49, 50, 15, 51,
        55,
    ),
    (
        3, 1, 76, 8, 77, 78, 0, 2, 79, 36, 37, 64, 4, 38, 9, 39, 65, 66, 40, 67, 41, 68, 42, 69,
        10, 70, 43, 32, 71, 24, 5, 56, 25, 57, 11, 26, 58, 27, 59, 33, 52, 34, 53, 35, 12, 60, 20, 54,
        28, 55, 29, 6, 61, 30, 62, 31, 63, 13, 21, 22, 80, 23, 48, 7, 14, 49, 50, 51, 15, 16, 17, 18,
        19,
    ),
    (
        2, 0, 3, 8, 1, 64, 65, 40, 41, 4, 66, 42, 67, 9, 43, 68, 36, 69, 32, 70, 33, 71, 34, 10,
        76, 35, 77, 37, 5, 78, 38, 79, 39, 11, 56, 28, 57, 16, 58, 17, 59, 18, 12, 60, 19, 61, 29, 62,
        30, 6, 52, 31, 63, 13, 53, 20, 21, 54, 22, 80, 55, 23, 7, 14, 24, 25, 26, 27, 15, 48, 49, 50,
        51,
    ),
    (
        3, 1, 0, 8, 2, 64, 65, 40, 41, 4, 66, 42, 67, 9, 43, 56, 36, 57, 37, 58, 38, 60, 39, 10,
        61, 24, 62, 25, 5, 63, 26, 68, 11, 69, 27, 28, 70, 29, 71, 20, 48, 30, 12, 49, 21, 50, 22, 51,
        23, 6, 52, 31, 53, 32, 54, 33, 13, 59, 34, 55, 35, 80, 76, 7, 14, 16, 77, 78, 17, 79, 18, 19,
        15,
    ),
)
ARRIVAL = (
    (
        11, 8, 9, 15, 10, 12, 13, 14,
    ),
    (
        11, 10, 9, 15, 12, 8, 13, 14,
    ),
    (
        12, 13, 15, 11, 10, 9, 14, 8,
    ),
    (
        12, 11, 15, 13, 10, 14, 9, 8,
    ),
    (
        12, 15, 13, 8, 9, 14, 10, 11,
    ),
    (
        10, 8, 13, 11, 12, 14, 15, 9,
    ),
    (
        13, 12, 9, 14, 8, 11, 15, 10,
    ),
    (
        8, 9, 13, 12, 10, 11, 15, 14,
    ),
    (
        11, 10, 13, 9, 8, 12, 14, 15,
    ),
    (
        10, 11, 13, 9, 8, 12, 14, 15,
    ),
    (
        13, 11, 12, 10, 8, 14, 15, 9,
    ),
    (
        15, 13, 12, 11, 14, 10, 8, 9,
    ),
    (
        13, 10, 14, 15, 11, 12, 8, 9,
    ),
    (
        14, 8, 15, 13, 9, 12, 11, 10,
    ),
    (
        9, 8, 10, 15, 13, 11, 12, 14,
    ),
    (
        9, 13, 10, 11, 8, 15, 12, 14,
    ),
)


def pick(values, row):
    value = jnp.int32(values[0])
    for c in range(1, len(values)):
        value = jnp.where(row == c, jnp.int32(values[c]), value)
    return value


def packed(codes, bits):
    return sum(code << (bits * i) for i, code in enumerate(codes))


def kernel(
    tokens, gain, weight, local, base, momentum,
    out, out_base, out_mom,
    tok, xg, gvec, wl, wr, prod, sbuf, rbuf, sq, sqr, rsf,
    bv, lv, mv, vbuf, frecv, fsum, xr, fown, fall,
    near_sem, far_sem, group_sem, load_sem, xs, xrs, zs, zr, qs, qr, fs, fr, hs, hr, gs, gr,
):
    rep = lax.axis_index("replica")
    t = lax.axis_index("tensor")
    f = lax.axis_index("fsdp")
    place = lax.rem(t + 4 * f, RING)
    row = f * RING + place
    other = (1 - f) * RING + lax.rem(place + 4, RING)
    y = rep // 4
    xh = lax.rem(rep // 2, 2)
    core = lax.rem(rep, 2)
    k = y * 2 + core

    def member(delta):
        p = lax.rem(k + delta, RING)
        return p, ((p // 2) * 4 + xh * 2 + lax.rem(p, 2), t, f)

    def on_ring(delta):
        return (rep, lax.rem(t + delta, RING), f)

    x_dev = (rep, t, 1 - f)
    h_dev = (y * 4 + (1 - xh) * 2 + core, t, f)

    def told(sem, count):
        @pl.when(count > 0)
        def _():
            pl.semaphore_wait(sem, count)

    barrier = pltpu.get_barrier_semaphore()
    pl.semaphore_signal(barrier, inc=1, device_id=x_dev, device_id_type=MESH)

    parts = [pick([codes[j] - 8 for codes in ARRIVAL], other) for j in range(8)]
    part_loads = [
        pltpu.make_async_copy(
            weight.at[0, :, pl.ds(pl.multiple_of(parts[j] * 128, 128), 128)], wl.at[parts[j]], load_sem.at[5 + j]
        )
        for j in range(8)
    ]
    for j in range(FIRST):
        part_loads[j].start()

    def on_pair(mine, theirs, sem, dev):
        @pl.when(mine < theirs if sem is barrier else mine > theirs)
        def _():
            pl.semaphore_signal(sem, inc=1, device_id=dev, device_id_type=MESH)

    def tell(near, far, group):
        for delta in range(1, RING):
            sem = near if delta in (1, RING - 1) else far
            on_pair(t, lax.rem(t + delta, RING), sem, on_ring(delta))
        for delta in range(1, RING):
            p, dev = member(delta)
            on_pair(k, p, group, dev)
        on_pair(xh, 1 - xh, group, h_dev)

    tell(barrier, barrier, barrier)
    loads = [
        pltpu.make_async_copy(src, dst, load_sem.at[i])
        for i, (src, dst) in enumerate(
            ((tokens, tok), (gain, gvec), (base, bv), (local.at[0], lv), (momentum, mv))
        )
    ]
    pl.semaphore_wait(barrier, 1 + t + k + xh)

    x_copies = []
    for j in range(8):
        x_copies.append(
            pltpu.make_async_remote_copy(
                src_ref=wl.at[parts[j]],
                dst_ref=wr.at[j],
                send_sem=xs.at[j],
                recv_sem=xrs.at[j],
                device_id=x_dev,
                device_id_type=MESH,
            )
        )
    for j in range(FIRST):
        part_loads[j].wait()
        x_copies[j].start()
    for load in loads + part_loads[FIRST:]:
        load.start()

    tell(near_sem, far_sem, group_sem)

    def sq_copy(delta):
        return pltpu.make_async_remote_copy(
            src_ref=sq, dst_ref=sqr.at[delta - 1], send_sem=qs.at[delta - 1], recv_sem=qr.at[delta - 1],
            device_id=on_ring(delta), device_id_type=MESH,
        )

    def rs_copy(delta):
        p, dev = member(delta)
        return pltpu.make_async_remote_copy(
            src_ref=vbuf.at[p], dst_ref=frecv.at[delta - 1], send_sem=fs.at[delta - 1],
            recv_sem=fr.at[delta - 1], device_id=dev, device_id_type=MESH,
        )

    def h_copy():
        return pltpu.make_async_remote_copy(
            src_ref=fsum, dst_ref=xr, send_sem=hs.at[0], recv_sem=hr.at[0], device_id=h_dev, device_id_type=MESH
        )

    core_dev = (y * 4 + xh * 2 + 1 - core, t, f)
    step_core = 1 - 2 * core

    def ag_copy(delta):
        return pltpu.make_async_remote_copy(
            src_ref=fown, dst_ref=fall.at[delta - 1], send_sem=gs.at[delta - 1], recv_sem=gr.at[delta - 1],
            device_id=member(delta)[1], device_id_type=MESH,
        )

    def core_copy(delta):
        slot = lax.rem(delta + step_core + RING, RING) - 1
        return pltpu.make_async_remote_copy(
            src_ref=fall.at[delta - 1] if delta else fown, dst_ref=fall.at[slot], send_sem=gs.at[delta],
            recv_sem=gr.at[slot], device_id=core_dev, device_id_type=MESH,
        )

    def z_copy(idx, h, dev):
        return pltpu.make_async_remote_copy(
            src_ref=sbuf.at[idx, h], dst_ref=rbuf.at[idx, h], send_sem=zs.at[idx * CUT + h],
            recv_sem=zr.at[idx * CUT + h], device_id=dev, device_id_type=MESH,
        )

    loads[2].wait()
    loads[3].wait()

    @pl.loop(0, RING)
    def _(p):
        for g in range(FCOLS // G):
            cols = pl.ds(pl.multiple_of(p * FCOLS + g * G, G), G)
            grad = bv[:, cols] - lv[:, cols]
            top = jnp.max(jnp.abs(grad), axis=1, keepdims=True)
            scale = (top + SCALE_EPS).astype(BF16).astype(F32)
            level = (grad / scale).astype(BF16).astype(F32)
            vbuf[p, :, g * G : (g + 1) * G] = (level * scale).astype(BF16)

    words = [
        pick([packed(codes[n : n + 4], 7) for codes in ORDER], row) for n in range(0, len(ORDER[0]), 4)
    ]
    arrival = pick([packed([u - 8 for u in parts], 3) for parts in ARRIVAL], row)

    loads[0].wait()
    loads[1].wait()

    @pl.loop(0, TOK // 128)
    def _(i):
        rows = pl.ds(pl.multiple_of(i * 128, 128), 128)
        xg[rows, :] = (tok[rows, :].astype(F32) * gvec[...]).astype(BF16)

    for j in range(FIRST, 8):
        part_loads[j].wait()

    @pl.when(t >= RING // 2)
    def _():
        for copy in x_copies[FIRST:]:
            copy.start()

    told(group_sem, RING - 1 - k + 1 - xh)
    for delta in range(1, RING):
        rs_copy(delta).start()

    near = jnp.where(t == 0, 2, jnp.where(t == RING - 1, 0, 1))
    told(near_sem, near)

    def own_product(q):
        both = jnp.concatenate([wl[2 * q], wl[2 * q + 1]], axis=1)
        res = jnp.dot(xg[...], both, preferred_element_type=F32)
        prod[2 * q] = res[:, :128].reshape(CUT, PART, 128)
        prod[2 * q + 1] = res[:, 128:].reshape(CUT, PART, 128)

    def other_product(j):
        pltpu.make_async_remote_copy(
            src_ref=wr.at[j], dst_ref=wr.at[j], send_sem=xs.at[j], recv_sem=xrs.at[j],
            device_id=x_dev, device_id_type=MESH,
        ).wait_recv()
        u = 8 + lax.bitwise_and(lax.shift_right_logical(arrival, 3 * j), jnp.int32(7))

        prod[u] = jnp.dot(xg[...], wr[j], preferred_element_type=F32).reshape(CUT, PART, 128)

    def pass_on(code):
        h = lax.rem(code, CUT)
        idx = code // CUT
        up = idx // 8
        r = lax.rem(idx, 8) // 2 + 1
        s = lax.rem(idx, 2)
        step = 2 * up - 1
        u = 2 * lax.rem(place + step * r + RING, RING) + s
        dev = on_ring(step + RING)
        first = (r == 4) | ((r == 3) & (s == 1 - up))

        @pl.when(first)
        def _():
            @pl.loop(0, PART // 128)
            def _(i):
                rows = pl.ds(pl.multiple_of(i * 128, 128), 128)
                sbuf[idx, h, rows, :] = prod[u, h, rows, :].astype(BF16)

        @pl.when(jnp.logical_not(first))
        def _():
            z_copy(idx + 2, h, dev).wait_recv()

            @pl.loop(0, PART // 128)
            def _(i):
                rows = pl.ds(pl.multiple_of(i * 128, 128), 128)
                sbuf[idx, h, rows, :] = (
                    prod[u, h, rows, :] + rbuf[idx + 2, h, rows, :].astype(F32)
                ).astype(BF16)

        z_copy(idx, h, dev).start()

    def squares():
        ones = jnp.ones((16, FEAT), BF16)
        sub = lax.broadcasted_iota(jnp.int32, (8, 128), 0)
        acc = jnp.zeros((8, 128), F32)
        for i in range(TOK // 256):
            x = tok[i * 256 : (i + 1) * 256, :].astype(F32)
            x2 = x * x
            hi = x2.astype(BF16)
            lo = (x2 - hi.astype(F32)).astype(BF16)
            dims = (((1,), (1,)), ((), ()))
            row = lax.dot_general(ones, hi, dims, preferred_element_type=F32)
            row = row + lax.dot_general(ones, lo, dims, preferred_element_type=F32)
            for g in range(2):
                acc = acc + jnp.where(sub == 2 * i + g, row[0:8, g * 128 : (g + 1) * 128], 0.0)
        sq[...] = acc
        told(far_sem, RING - 1 - t - near)
        for delta in range(1, RING):
            sq_copy(delta).start()

    def fragment_sum():
        for delta in range(1, RING):
            rs_copy(delta).wait_recv()
        total = vbuf[k].astype(F32)
        for delta in range(1, RING):
            total = total + frecv[delta - 1].astype(F32)
        fsum[...] = total.astype(BF16)
        h_copy().start()

        @pl.when(t < RING // 2)
        def _():
            for copy in x_copies[FIRST:]:
                copy.start()

    def fragment_spread():
        h_copy().wait_recv()
        fown[...] = (fsum[...].astype(F32) + xr[...].astype(F32)).astype(BF16)
        for delta in (2, 4, 6):
            ag_copy(delta).start()
        core_copy(0).start()

    def fragment_pass():
        for delta in (2, 4, 6):
            ag_copy(delta).wait_recv()
            core_copy(delta).start()

    def fragment_end():
        for delta in (1, 3, 5, 7):
            ag_copy(delta).wait_recv()
        loads[4].wait()

        for delta in range(RING):
            p = lax.rem(k + RING - delta, RING)
            cols = pl.ds(pl.multiple_of(p * FCOLS, FCOLS), FCOLS)
            piece = fown[...] if delta == 0 else fall[delta - 1]
            average = piece.astype(F32) / REPLICAS
            new_mom = OUTER_MOMENTUM * mv[:, cols] + average
            out_mom[:, cols] = new_mom
            out_base[:, cols] = bv[:, cols] - OUTER_RATE * (average + OUTER_MOMENTUM * new_mom)

        total = sq[...]
        for delta in range(1, RING):
            sq_copy(delta).wait_recv()
            total = total + sqr[delta - 1]
        rs = lax.rsqrt(total / WIDTH + NORM_EPS)
        for g in range(TOK // 128):
            rsf[g * 128 // PART, g * 128 % PART : g * 128 % PART + 128, :] = jnp.broadcast_to(rs[g : g + 1, :], (128, 128)).T

    @pl.loop(0, len(ORDER[0]))
    def _(n):
        word = words[0]
        for i in range(1, len(words)):
            word = jnp.where(n // 4 == i, words[i], word)
        code = lax.bitwise_and(lax.shift_right_logical(word, 7 * lax.rem(n, 4)), jnp.int32(127))

        @pl.when(code < 4)
        def _():
            own_product(code)

        @pl.when((code >= 8) & (code < 16))
        def _():
            other_product(code - 8)

        @pl.when((code >= 16) & (code < 16 + 16 * CUT))
        def _():
            pass_on(code - 16)

        @pl.when(code == 4)
        def _():
            squares()

        @pl.when(code == 5)
        def _():
            fragment_sum()

        @pl.when(code == 6)
        def _():
            fragment_spread()

        @pl.when(code == 7)
        def _():
            fragment_end()

        @pl.when(code == 16 + 16 * CUT)
        def _():
            fragment_pass()

    for h in range(CUT):
        for s in range(2):
            z_copy(s, h, on_ring(1)).wait_recv()
            z_copy(8 + s, h, on_ring(1)).wait_recv()

            @pl.loop(0, PART // 128)
            def _(i):
                rows = pl.ds(pl.multiple_of(i * 128, 128), 128)
                total = prod[2 * place + s, h, rows, :] + rbuf[s, h, rows, :].astype(F32)
                total = total + rbuf[8 + s, h, rows, :].astype(F32)
                out[pl.ds(pl.multiple_of(h * PART + i * 128, 128), 128), s * 128 : (s + 1) * 128] = (total * rsf[h, rows, :]).astype(BF16)

    for copy in x_copies:
        copy.wait_send()
    for idx in range(16):
        if idx in (6 + 1, 8 + 6):
            continue
        for h in range(CUT):
            z_copy(idx, h, on_ring(1)).wait_send()
    for delta in range(1, RING):
        sq_copy(delta).wait_send()
        rs_copy(delta).wait_send()
    for delta in (2, 4, 6):
        ag_copy(delta).wait_send()
        core_copy(delta).wait_send()
    core_copy(0).wait_send()
    h_copy().wait_send()


def write_out(a, b, c, a_out, b_out, c_out, sem):
    copies = []
    for src, dst in ((a, a_out), (b, b_out), (c, c_out)):
        rows = src.shape[0] // 2
        for i in range(2):
            part = pl.ds(i * rows, rows)
            copies.append(pltpu.make_async_copy(src.at[part], dst.at[part], sem.at[len(copies)]))
            copies[-1].start()
    for copy in copies:
        copy.wait()


def body(tokens, gain, weight, local, base, momentum):
    dma = pltpu.SemaphoreType.DMA
    any_spec = pl.BlockSpec(memory_space=pltpu.HBM)
    parts = pl.pallas_call(
        kernel,
        out_shape=(
            pltpu.VMEM((TOK, 256), BF16),
            pltpu.VMEM(base.shape, F32),
            pltpu.VMEM(base.shape, F32),
        ),
        in_specs=[any_spec] * 6,
        out_specs=[pl.BlockSpec(memory_space=pltpu.VMEM)] * 3,
        scratch_shapes=[
            pltpu.VMEM((TOK, FEAT), BF16),
            pltpu.VMEM((TOK, FEAT), BF16),
            pltpu.VMEM((1, FEAT), F32),
            pltpu.VMEM((8, FEAT, 128), BF16),
            pltpu.VMEM((8, FEAT, 128), BF16),
            pltpu.VMEM((16, CUT, PART, 128), F32),
            pltpu.VMEM((16, CUT, PART, 128), BF16),
            pltpu.VMEM((16, CUT, PART, 128), BF16),
            pltpu.VMEM((8, 128), F32),
            pltpu.VMEM((RING - 1, 8, 128), F32),
            pltpu.VMEM((CUT, PART, 128), F32),
            pltpu.VMEM((FROWS, WIDTH), F32),
            pltpu.VMEM((FROWS, WIDTH), F32),
            pltpu.VMEM((FROWS, WIDTH), F32),
            pltpu.VMEM((RING, FROWS, FCOLS), BF16),
            pltpu.VMEM((RING - 1, FROWS, FCOLS), BF16),
            pltpu.VMEM((FROWS, FCOLS), BF16),
            pltpu.VMEM((FROWS, FCOLS), BF16),
            pltpu.VMEM((FROWS, FCOLS), BF16),
            pltpu.VMEM((RING - 1, FROWS, FCOLS), BF16),
            pltpu.SemaphoreType.REGULAR,
            pltpu.SemaphoreType.REGULAR,
            pltpu.SemaphoreType.REGULAR,
            dma((5 + 8,)),
            dma((8,)),
            dma((8,)),
            dma((16 * CUT,)),
            dma((16 * CUT,)),
            dma((RING - 1,)),
            dma((RING - 1,)),
            dma((RING - 1,)),
            dma((RING - 1,)),
            dma((1,)),
            dma((1,)),
            dma((RING - 1,)),
            dma((RING - 1,)),
        ],
        compiler_params=pltpu.CompilerParams(
            collective_id=0, has_side_effects=True, vmem_limit_bytes=50 * 1024 * 1024
        ),
    )(tokens, gain.reshape(1, FEAT), weight, local, base, momentum)
    return pl.pallas_call(
        write_out,
        out_shape=tuple(jax.ShapeDtypeStruct(part.shape, part.dtype) for part in parts),
        in_specs=[pl.BlockSpec(memory_space=pl.ANY)] * 3,
        out_specs=[any_spec] * 3,
        scratch_shapes=[dma((6,))],
        compiler_params=pltpu.CompilerParams(vmem_limit_bytes=1024 * 1024),
    )(*parts)


def solution(mesh):
    placed = (
        P(("replica", "fsdp"), "tensor"),
        P("tensor"),
        P("replica", "tensor", "fsdp"),
        P("replica", ("tensor", "fsdp"), None),
        P(("tensor", "fsdp"), None),
        P(("tensor", "fsdp"), None),
    )
    return jax.shard_map(
        body,
        mesh=mesh,
        in_specs=placed,
        out_specs=(
            P(("replica", "fsdp"), "tensor"),
            P(("tensor", "fsdp"), None),
            P(("tensor", "fsdp"), None),
        ),
        check_vma=False,
    )
```

time: 75.8 us -> 70.5 us (0.930)
  the two profiles are of different devices: /device:TPU:6 before, /device:TPU:1 now
where the time goes in v3:
time: 70.5 us; the launch traced here: 70.3 us
  Pallas kernels  69 us (98%)
    pallas_call x1, Pallas kernels, body(): pl.pallas_call(kernel, out_shape=(pltpu.VMEM((TOK, 256), BF16), pltpu.VME...  67.1 us
    pallas_call x1, Pallas kernels, body(): pl.pallas_call(write_out, out_shape=tuple((jax.ShapeDtypeStruct(part.shap...  1.88 us

profile of v3, /device:TPU:1, one launch (start us, length us, event | category | flops | bytes accessed | tf_op | source)
XLA Modules:
  0.0 70.3 jit_solution(2112776928001193538)
XLA Ops:
  0.6 0.0 copy-start
  0.6 0.7 copy-done
  1.3 67.1 %shard_map.85 = (bf16[1024,256]{1,0:T(8,128)(2,1)S(1)}, f32[48,8192]{1,0:T(8,128)S(1)}, f32[48,8192]{1,0:T(8,128)S(1)}) custom-call(bf16[1024,1024]{1,0:T(8,128)(2,1)} %tokens.1, f32[1,1024]{1,0:T(1,128)S(1)} %bitcast.1, bf16[1,1024,1024]{2,1,0:T(8,128)(2,1)} %weight.1, f32[1,48,8192]{2,1,0:T(8,128)} %local.1, f32[48,8192]{1,0:T(8,128)} %base.1, ...), custom_call_target="tpu_custom_call" | custom-call | tf_op jit(solution)/shard_map/pallas_call | solution.py:556
  68.5 1.9 %shard_map.86 = (bf16[1024,256]{1,0:T(8,128)(2,1)}, f32[48,8192]{1,0:T(8,128)}, f32[48,8192]{1,0:T(8,128)}) custom-call(bf16[1024,256]{1,0:T(8,128)(2,1)S(1)} %get-tuple-element.6.a, f32[48,8192]{1,0:T(8,128)S(1)} %get-tuple-element.7.b, f32[48,8192]{1,0:T(8,128)S(1)} %get-tuple-element.8.c), custom_call_target="tpu_custom_call" | custom-call | tf_op jit(solution)/shard_map/pallas_call | solution.py:607
Async XLA Ops:
  0.6 0.7 copy-start

commit v4 on v3

--- a/solution.py
+++ b/solution.py
@@ -28,150 +28,150 @@
 
 ORDER = (
     (
-        8, 0, 3, 2, 1, 36, 37, 64, 65, 9, 40, 66, 4, 41, 67, 42, 43, 68, 10, 76, 77, 38, 39, 78,
-        5, 79, 56, 11, 57, 58, 59, 69, 20, 12, 32, 33, 70, 71, 34, 48, 35, 6, 49, 60, 13, 61, 24, 25,
-        62, 21, 80, 63, 26, 50, 7, 14, 51, 27, 22, 52, 53, 23, 54, 15, 28, 55, 29, 30, 31, 16, 17, 18,
-        19,
-    ),
-    (
-        2, 1, 0, 8, 76, 77, 3, 78, 4, 79, 9, 40, 41, 56, 42, 57, 43, 58, 10, 59, 20, 60, 21, 68,
-        5, 22, 69, 16, 11, 70, 28, 71, 23, 48, 17, 49, 18, 50, 12, 19, 32, 51, 33, 61, 29, 62, 6, 34,
-        63, 30, 31, 13, 64, 65, 35, 66, 80, 67, 7, 14, 36, 37, 52, 53, 38, 54, 39, 55, 15, 24, 25, 26,
-        27,
-    ),
-    (
-        2, 0, 1, 8, 3, 40, 41, 4, 42, 43, 9, 76, 77, 28, 78, 29, 79, 30, 48, 10, 49, 24, 36, 50,
-        31, 51, 5, 25, 52, 26, 11, 68, 27, 69, 37, 70, 20, 71, 38, 12, 64, 39, 65, 21, 66, 22, 6, 67,
-        23, 53, 16, 54, 13, 55, 17, 18, 60, 80, 19, 61, 62, 7, 14, 32, 33, 63, 34, 35, 15, 56, 57, 58,
-        59,
-    ),
-    (
-        0, 1, 3, 8, 2, 64, 65, 36, 37, 4, 66, 38, 67, 9, 32, 39, 33, 34, 35, 10, 76, 77, 20, 78,
-        28, 5, 79, 21, 22, 11, 68, 69, 23, 70, 29, 71, 30, 60, 31, 12, 61, 24, 62, 25, 63, 26, 6, 56,
-        27, 57, 16, 58, 13, 59, 40, 41, 42, 80, 43, 7, 14, 17, 52, 18, 53, 54, 19, 55, 15, 48, 49, 50,
-        51,
-    ),
-    (
-        3, 2, 0, 8, 40, 41, 1, 42, 76, 77, 4, 43, 56, 9, 28, 57, 36, 58, 29, 59, 30, 78, 31, 10,
-        79, 37, 38, 68, 5, 39, 69, 70, 32, 11, 71, 33, 34, 60, 35, 61, 24, 62, 12, 20, 63, 21, 22, 23,
-        13, 64, 65, 25, 66, 16, 67, 26, 27, 14, 48, 49, 17, 18, 50, 19, 51, 15, 52, 53, 54, 55, 6, 80,
-        7,
-    ),
-    (
-        2, 0, 3, 8, 1, 36, 37, 64, 65, 4, 38, 66, 39, 9, 68, 40, 67, 41, 69, 42, 76, 43, 77, 10,
-        24, 78, 25, 79, 5, 26, 70, 32, 71, 11, 28, 29, 30, 31, 12, 48, 49, 27, 33, 50, 34, 51, 35, 52,
-        13, 53, 16, 17, 54, 18, 55, 19, 56, 14, 57, 58, 59, 60, 15, 61, 20, 21, 62, 22, 63, 23, 6, 80,
-        7,
-    ),
-    (
-        3, 1, 0, 8, 2, 76, 77, 36, 37, 4, 78, 38, 79, 9, 39, 56, 32, 57, 33, 58, 34, 64, 40, 10,
-        59, 28, 65, 29, 5, 68, 30, 69, 31, 11, 70, 35, 71, 41, 66, 42, 67, 43, 12, 60, 24, 61, 25, 62,
-        26, 63, 27, 13, 20, 21, 14, 22, 23, 48, 49, 15, 16, 50, 17, 18, 51, 19, 52, 6, 53, 54, 55, 80,
-        7,
-    ),
-    (
-        3, 0, 1, 8, 2, 76, 77, 40, 41, 4, 78, 42, 79, 9, 36, 64, 37, 65, 38, 66, 39, 67, 43, 10,
-        48, 32, 49, 33, 5, 50, 34, 56, 35, 11, 51, 57, 68, 69, 12, 70, 24, 25, 71, 26, 58, 27, 59, 13,
-        28, 29, 60, 61, 30, 62, 31, 63, 16, 14, 17, 52, 53, 18, 54, 19, 55, 15, 20, 21, 6, 22, 23, 80,
-        7,
-    ),
-    (
-        1, 3, 0, 8, 2, 36, 37, 64, 65, 4, 38, 66, 39, 9, 67, 32, 56, 33, 57, 34, 58, 35, 48, 10,
-        49, 50, 5, 52, 28, 53, 11, 29, 76, 30, 77, 31, 78, 79, 12, 40, 41, 60, 42, 61, 43, 62, 63, 13,
-        54, 55, 59, 24, 25, 14, 51, 26, 27, 68, 16, 17, 15, 69, 18, 70, 19, 71, 20, 6, 21, 22, 23, 80,
-        7,
-    ),
-    (
-        3, 1, 2, 8, 40, 41, 0, 42, 4, 43, 9, 76, 77, 78, 79, 20, 56, 21, 10, 36, 37, 48, 49, 38,
-        50, 5, 39, 57, 22, 11, 23, 58, 59, 16, 17, 18, 12, 64, 65, 19, 66, 67, 68, 13, 32, 33, 69, 70,
-        34, 71, 35, 52, 14, 24, 25, 53, 54, 26, 51, 27, 55, 15, 28, 29, 60, 30, 31, 61, 6, 62, 63, 80,
-        7,
-    ),
-    (
-        0, 2, 3, 8, 1, 76, 77, 4, 78, 79, 9, 28, 29, 30, 68, 31, 69, 10, 24, 40, 70, 25, 71, 5,
-        26, 48, 27, 11, 64, 65, 41, 42, 66, 43, 67, 49, 16, 12, 50, 17, 51, 18, 20, 56, 57, 13, 32, 33,
-        58, 34, 59, 35, 14, 36, 37, 38, 19, 39, 15, 60, 61, 21, 22, 62, 23, 63, 6, 52, 53, 54, 55, 80,
-        7,
-    ),
-    (
-        2, 3, 0, 8, 1, 36, 37, 76, 77, 4, 38, 78, 39, 9, 79, 32, 68, 33, 69, 34, 70, 35, 71, 10,
-        20, 64, 21, 65, 5, 22, 66, 23, 67, 11, 24, 60, 25, 61, 26, 62, 28, 63, 12, 40, 41, 42, 43, 13,
-        56, 57, 16, 17, 58, 27, 59, 18, 14, 48, 49, 29, 30, 50, 31, 51, 19, 15, 52, 6, 53, 54, 55, 80,
-        7,
-    ),
-    (
-        8, 0, 40, 41, 1, 42, 2, 3, 43, 9, 76, 77, 36, 4, 28, 78, 37, 79, 29, 10, 30, 64, 65, 31,
-        66, 38, 5, 67, 39, 60, 11, 61, 32, 33, 68, 34, 62, 16, 63, 17, 12, 69, 18, 70, 19, 71, 35, 6,
-        52, 24, 53, 25, 54, 13, 20, 56, 26, 57, 80, 21, 58, 22, 7, 14, 59, 48, 23, 27, 49, 50, 15, 51,
-        55,
-    ),
-    (
-        3, 1, 76, 8, 77, 78, 0, 2, 79, 36, 37, 64, 4, 38, 9, 39, 65, 66, 40, 67, 41, 68, 42, 69,
-        10, 70, 43, 32, 71, 24, 5, 56, 25, 57, 11, 26, 58, 27, 59, 33, 52, 34, 53, 35, 12, 60, 20, 54,
-        28, 55, 29, 6, 61, 30, 62, 31, 63, 13, 21, 22, 80, 23, 48, 7, 14, 49, 50, 51, 15, 16, 17, 18,
-        19,
-    ),
-    (
-        2, 0, 3, 8, 1, 64, 65, 40, 41, 4, 66, 42, 67, 9, 43, 68, 36, 69, 32, 70, 33, 71, 34, 10,
-        76, 35, 77, 37, 5, 78, 38, 79, 39, 11, 56, 28, 57, 16, 58, 17, 59, 18, 12, 60, 19, 61, 29, 62,
-        30, 6, 52, 31, 63, 13, 53, 20, 21, 54, 22, 80, 55, 23, 7, 14, 24, 25, 26, 27, 15, 48, 49, 50,
-        51,
-    ),
-    (
-        3, 1, 0, 8, 2, 64, 65, 40, 41, 4, 66, 42, 67, 9, 43, 56, 36, 57, 37, 58, 38, 60, 39, 10,
-        61, 24, 62, 25, 5, 63, 26, 68, 11, 69, 27, 28, 70, 29, 71, 20, 48, 30, 12, 49, 21, 50, 22, 51,
-        23, 6, 52, 31, 53, 32, 54, 33, 13, 59, 34, 55, 35, 80, 76, 7, 14, 16, 77, 78, 17, 79, 18, 19,
-        15,
+        0, 8, 1, 3, 64, 65, 2, 66, 4, 9, 67, 76, 40, 41, 77, 42, 78, 43, 68, 10, 85, 69, 32, 33,
+        70, 34, 79, 5, 35, 60, 11, 36, 61, 37, 62, 38, 71, 39, 63, 12, 24, 56, 25, 57, 26, 58, 27, 6,
+        48, 59, 52, 13, 49, 53, 80, 50, 7, 14, 51, 54, 28, 29, 55, 30, 31, 81, 82, 83, 84, 20, 21, 22,
+        23, 16, 17, 18, 19,
+    ),
+    (
+        2, 3, 1, 8, 0, 76, 77, 4, 78, 56, 9, 40, 57, 41, 42, 58, 43, 59, 79, 10, 32, 33, 85, 34,
+        60, 35, 5, 20, 61, 11, 21, 62, 68, 22, 69, 23, 70, 71, 12, 16, 64, 63, 17, 65, 6, 18, 66, 19,
+        67, 48, 13, 36, 49, 37, 38, 50, 80, 39, 51, 52, 7, 14, 28, 29, 53, 54, 30, 55, 31, 81, 82, 83,
+        84, 24, 25, 26, 27,
+    ),
+    (
+        2, 1, 0, 8, 3, 40, 41, 4, 42, 43, 9, 68, 69, 28, 70, 29, 48, 30, 49, 31, 10, 64, 20, 85,
+        65, 21, 66, 22, 5, 67, 23, 11, 50, 24, 51, 36, 71, 25, 52, 26, 12, 76, 27, 77, 37, 78, 38, 6,
+        79, 16, 53, 39, 54, 17, 13, 32, 55, 33, 80, 34, 35, 7, 14, 60, 61, 18, 19, 62, 63, 81, 82, 83,
+        84, 56, 57, 58, 59,
+    ),
+    (
+        3, 1, 0, 8, 2, 36, 37, 4, 38, 76, 77, 39, 9, 78, 28, 79, 29, 30, 31, 10, 32, 64, 65, 85,
+        33, 66, 34, 67, 5, 35, 56, 11, 57, 40, 41, 58, 42, 59, 24, 12, 43, 25, 16, 68, 6, 17, 69, 18,
+        70, 19, 13, 71, 60, 26, 61, 27, 80, 62, 20, 63, 21, 7, 14, 22, 23, 52, 53, 81, 82, 83, 84, 54,
+        55, 48, 49, 50, 51,
+    ),
+    (
+        0, 3, 1, 8, 36, 37, 2, 38, 76, 77, 4, 39, 78, 9, 68, 40, 41, 79, 42, 69, 43, 70, 28, 10,
+        71, 85, 32, 33, 34, 5, 29, 11, 56, 57, 35, 58, 24, 59, 25, 26, 12, 48, 27, 49, 50, 30, 51, 31,
+        20, 13, 16, 64, 65, 17, 66, 18, 67, 19, 60, 14, 21, 61, 22, 62, 23, 63, 81, 82, 83, 84, 52, 53,
+        54, 55, 6, 80, 7,
+    ),
+    (
+        0, 3, 1, 8, 76, 77, 2, 78, 36, 37, 4, 79, 38, 9, 68, 39, 64, 40, 69, 41, 70, 42, 65, 10,
+        28, 85, 71, 43, 66, 32, 67, 33, 5, 34, 11, 60, 61, 35, 62, 29, 63, 30, 48, 31, 12, 49, 24, 50,
+        25, 51, 26, 27, 13, 56, 14, 16, 17, 57, 58, 18, 59, 19, 52, 20, 53, 81, 82, 83, 84, 54, 21, 22,
+        55, 23, 6, 80, 7,
+    ),
+    (
+        2, 1, 3, 8, 76, 77, 0, 78, 40, 41, 4, 79, 42, 9, 43, 68, 69, 36, 70, 32, 71, 33, 60, 10,
+        34, 85, 64, 35, 61, 37, 62, 38, 5, 65, 39, 11, 63, 66, 67, 16, 52, 17, 12, 53, 18, 54, 19, 55,
+        20, 56, 13, 24, 25, 57, 26, 58, 27, 59, 28, 14, 29, 30, 31, 21, 81, 82, 83, 84, 48, 49, 22, 50,
+        51, 6, 23, 80, 7,
+    ),
+    (
+        0, 1, 3, 8, 2, 76, 77, 4, 78, 40, 41, 68, 9, 42, 69, 43, 70, 71, 79, 10, 32, 33, 64, 85,
+        34, 65, 35, 66, 5, 24, 67, 11, 56, 25, 26, 60, 27, 61, 28, 57, 12, 16, 62, 17, 58, 18, 59, 19,
+        63, 13, 36, 52, 37, 53, 38, 54, 39, 48, 14, 49, 29, 30, 50, 20, 51, 21, 55, 81, 82, 83, 84, 22,
+        23, 31, 6, 80, 7,
+    ),
+    (
+        0, 1, 3, 8, 40, 41, 2, 42, 64, 65, 4, 43, 66, 9, 67, 56, 57, 58, 10, 68, 32, 33, 69, 85,
+        34, 70, 35, 48, 5, 49, 11, 36, 37, 50, 38, 51, 39, 71, 59, 12, 28, 29, 60, 30, 31, 24, 13, 76,
+        77, 25, 78, 26, 79, 27, 61, 14, 62, 63, 16, 17, 81, 82, 18, 83, 84, 52, 19, 53, 20, 6, 21, 54,
+        22, 55, 23, 80, 7,
+    ),
+    (
+        2, 1, 0, 8, 3, 76, 77, 4, 78, 79, 9, 40, 41, 56, 42, 57, 43, 58, 16, 59, 10, 48, 20, 85,
+        17, 49, 21, 50, 5, 18, 60, 11, 36, 61, 37, 62, 38, 39, 12, 32, 64, 65, 33, 66, 34, 63, 35, 51,
+        13, 52, 22, 23, 67, 19, 24, 14, 25, 68, 69, 26, 70, 27, 71, 53, 81, 28, 82, 29, 83, 30, 84, 54,
+        55, 31, 6, 80, 7,
+    ),
+    (
+        2, 1, 0, 8, 76, 77, 3, 78, 4, 79, 9, 24, 64, 65, 28, 66, 25, 67, 29, 10, 48, 26, 68, 85,
+        27, 49, 50, 5, 51, 11, 40, 41, 69, 42, 70, 43, 71, 30, 52, 12, 31, 53, 54, 56, 13, 32, 33, 57,
+        58, 34, 55, 35, 14, 36, 37, 59, 38, 39, 20, 81, 60, 82, 61, 83, 62, 84, 21, 22, 63, 23, 6, 16,
+        17, 18, 19, 80, 7,
+    ),
+    (
+        0, 3, 1, 8, 2, 32, 76, 77, 36, 4, 33, 78, 37, 79, 9, 34, 35, 20, 56, 21, 10, 64, 65, 22,
+        85, 66, 23, 67, 38, 5, 57, 39, 11, 68, 69, 70, 16, 71, 12, 40, 41, 58, 59, 42, 43, 17, 13, 18,
+        60, 61, 19, 62, 28, 63, 29, 14, 48, 49, 30, 31, 50, 24, 51, 25, 81, 82, 83, 84, 26, 27, 52, 6,
+        53, 54, 55, 80, 7,
+    ),
+    (
+        1, 8, 0, 2, 3, 40, 41, 4, 9, 42, 43, 76, 77, 28, 78, 29, 79, 30, 68, 10, 31, 85, 64, 20,
+        65, 21, 66, 5, 22, 67, 11, 23, 69, 16, 70, 24, 71, 17, 12, 56, 57, 18, 19, 58, 25, 59, 6, 26,
+        60, 27, 61, 36, 13, 62, 37, 63, 38, 48, 80, 39, 49, 7, 14, 50, 51, 32, 33, 52, 34, 53, 35, 54,
+        81, 82, 83, 84, 55,
+    ),
+    (
+        2, 0, 3, 8, 1, 64, 65, 36, 37, 4, 66, 38, 67, 9, 39, 76, 28, 77, 29, 68, 30, 69, 31, 10,
+        70, 85, 24, 71, 32, 78, 25, 5, 79, 26, 11, 56, 27, 57, 33, 58, 34, 59, 35, 12, 60, 20, 61, 16,
+        62, 17, 6, 63, 18, 48, 19, 49, 40, 13, 52, 41, 53, 42, 80, 54, 43, 55, 7, 14, 50, 21, 22, 51,
+        81, 82, 83, 84, 23,
+    ),
+    (
+        1, 2, 3, 8, 36, 37, 0, 38, 76, 77, 4, 39, 78, 9, 79, 32, 40, 64, 33, 65, 34, 66, 35, 10,
+        85, 41, 67, 60, 42, 56, 43, 5, 61, 28, 11, 62, 24, 63, 25, 57, 26, 58, 27, 48, 12, 16, 49, 17,
+        50, 18, 51, 6, 19, 52, 29, 53, 30, 13, 54, 20, 55, 21, 59, 80, 22, 68, 7, 14, 23, 31, 69, 70,
+        71, 81, 82, 83, 84,
+    ),
+    (
+        3, 2, 0, 8, 40, 41, 1, 42, 64, 65, 4, 43, 66, 9, 36, 67, 37, 76, 38, 77, 39, 78, 32, 10,
+        56, 85, 57, 33, 34, 58, 35, 59, 5, 79, 11, 24, 52, 25, 68, 26, 53, 27, 54, 12, 28, 55, 29, 69,
+        30, 70, 31, 6, 71, 20, 48, 21, 13, 22, 49, 50, 23, 80, 16, 17, 7, 14, 18, 19, 51, 60, 61, 81,
+        82, 83, 84, 62, 63,
     ),
 )
 ARRIVAL = (
     (
-        11, 8, 9, 15, 10, 12, 13, 14,
-    ),
-    (
-        11, 10, 9, 15, 12, 8, 13, 14,
-    ),
-    (
-        12, 13, 15, 11, 10, 9, 14, 8,
-    ),
-    (
-        12, 11, 15, 13, 10, 14, 9, 8,
-    ),
-    (
-        12, 15, 13, 8, 9, 14, 10, 11,
-    ),
-    (
-        10, 8, 13, 11, 12, 14, 15, 9,
-    ),
-    (
-        13, 12, 9, 14, 8, 11, 15, 10,
-    ),
-    (
-        8, 9, 13, 12, 10, 11, 15, 14,
-    ),
-    (
-        11, 10, 13, 9, 8, 12, 14, 15,
-    ),
-    (
-        10, 11, 13, 9, 8, 12, 14, 15,
-    ),
-    (
-        13, 11, 12, 10, 8, 14, 15, 9,
-    ),
-    (
-        15, 13, 12, 11, 14, 10, 8, 9,
-    ),
-    (
-        13, 10, 14, 15, 11, 12, 8, 9,
-    ),
-    (
-        14, 8, 15, 13, 9, 12, 11, 10,
-    ),
-    (
-        9, 8, 10, 15, 13, 11, 12, 14,
-    ),
-    (
-        9, 13, 10, 11, 8, 15, 12, 14,
+        9, 8, 10, 11, 12, 13, 15, 14,
+    ),
+    (
+        11, 10, 12, 9, 8, 13, 15, 14,
+    ),
+    (
+        12, 11, 10, 15, 13, 14, 9, 8,
+    ),
+    (
+        15, 10, 12, 14, 13, 11, 9, 8,
+    ),
+    (
+        13, 15, 9, 12, 10, 14, 8, 11,
+    ),
+    (
+        13, 12, 14, 15, 11, 9, 8, 10,
+    ),
+    (
+        10, 15, 9, 13, 11, 8, 12, 14,
+    ),
+    (
+        10, 12, 8, 11, 13, 9, 15, 14,
+    ),
+    (
+        8, 12, 10, 11, 13, 9, 14, 15,
+    ),
+    (
+        11, 10, 12, 13, 8, 14, 9, 15,
+    ),
+    (
+        13, 10, 11, 12, 8, 14, 15, 9,
+    ),
+    (
+        15, 10, 12, 13, 14, 11, 8, 9,
+    ),
+    (
+        15, 13, 14, 9, 12, 10, 11, 8,
+    ),
+    (
+        9, 12, 8, 14, 15, 13, 11, 10,
+    ),
+    (
+        15, 8, 9, 14, 10, 11, 13, 12,
+    ),
+    (
+        9, 8, 10, 11, 13, 12, 15, 14,
     ),
 )
 
@@ -181,6 +181,10 @@
     for c in range(1, len(values)):
         value = jnp.where(row == c, jnp.int32(values[c]), value)
     return value
+
+
+def low(value, size):
+    return lax.bitwise_and(value, jnp.int32(size - 1))
 
 
 def packed(codes, bits):
@@ -330,7 +334,7 @@
             vbuf[p, :, g * G : (g + 1) * G] = (level * scale).astype(BF16)
 
     words = [
-        pick([packed(codes[n : n + 4], 7) for codes in ORDER], row) for n in range(0, len(ORDER[0]), 4)
+        pick([packed((codes[n : n + 4] + (127,) * 3)[:4], 7) for codes in ORDER], row) for n in range(0, len(ORDER[0]), 4)
     ]
     arrival = pick([packed([u - 8 for u in parts], 3) for parts in ARRIVAL], row)
 
@@ -340,7 +344,7 @@
     @pl.loop(0, TOK // 128)
     def _(i):
         rows = pl.ds(pl.multiple_of(i * 128, 128), 128)
-        xg[rows, :] = (tok[rows, :].astype(F32) * gvec[...]).astype(BF16)
+        xg[rows, :] = (tok[rows, :].astype(F32) * gvec[...].reshape(1, FEAT)).astype(BF16)
 
     for j in range(FIRST, 8):
         part_loads[j].wait()
@@ -372,34 +376,35 @@
 
         prod[u] = jnp.dot(xg[...], wr[j], preferred_element_type=F32).reshape(CUT, PART, 128)
 
+    def last_product(h):
+        @pl.when(h == 0)
+        def _():
+            x_copies[7].wait_recv()
+
+        u = 8 + lax.bitwise_and(lax.shift_right_logical(arrival, 21), jnp.int32(7))
+        rows = pl.ds(pl.multiple_of(h * PART, PART), PART)
+        prod[u, h] = jnp.dot(xg[rows, :], wr[7], preferred_element_type=F32)
+
     def pass_on(code):
-        h = lax.rem(code, CUT)
-        idx = code // CUT
-        up = idx // 8
-        r = lax.rem(idx, 8) // 2 + 1
-        s = lax.rem(idx, 2)
+        h = low(code, CUT)
+        idx = lax.shift_right_logical(code, CUT.bit_length() - 1)
+        up = lax.shift_right_logical(idx, 3)
+        r = lax.shift_right_logical(low(idx, 8), 1) + 1
+        s = low(idx, 2)
         step = 2 * up - 1
-        u = 2 * lax.rem(place + step * r + RING, RING) + s
-        dev = on_ring(step + RING)
+        u = 2 * low(place + step * r + RING, RING) + s
+        dev = (rep, low(t + step + RING, RING), f)
         first = (r == 4) | ((r == 3) & (s == 1 - up))
 
         @pl.when(first)
         def _():
-            @pl.loop(0, PART // 128)
-            def _(i):
-                rows = pl.ds(pl.multiple_of(i * 128, 128), 128)
-                sbuf[idx, h, rows, :] = prod[u, h, rows, :].astype(BF16)
+            sbuf[idx, h] = prod[u, h].astype(BF16)
 
         @pl.when(jnp.logical_not(first))
         def _():
             z_copy(idx + 2, h, dev).wait_recv()
 
-            @pl.loop(0, PART // 128)
-            def _(i):
-                rows = pl.ds(pl.multiple_of(i * 128, 128), 128)
-                sbuf[idx, h, rows, :] = (
-                    prod[u, h, rows, :] + rbuf[idx + 2, h, rows, :].astype(F32)
-                ).astype(BF16)
+            sbuf[idx, h] = (prod[u, h] + rbuf[idx + 2, h].astype(F32)).astype(BF16)
 
         z_copy(idx, h, dev).start()
 
@@ -462,6 +467,7 @@
             out_mom[:, cols] = new_mom
             out_base[:, cols] = bv[:, cols] - OUTER_RATE * (average + OUTER_MOMENTUM * new_mom)
 
+    def row_scale():
         total = sq[...]
         for delta in range(1, RING):
             sq_copy(delta).wait_recv()
@@ -470,56 +476,68 @@
         for g in range(TOK // 128):
             rsf[g * 128 // PART, g * 128 % PART : g * 128 % PART + 128, :] = jnp.broadcast_to(rs[g : g + 1, :], (128, 128)).T
 
-    @pl.loop(0, len(ORDER[0]))
+    def do(code):
+        sends = (code >= 16) & (code < 16 + 16 * CUT)
+
+        @pl.when(sends)
+        def _():
+            pass_on(code - 16)
+
+        @pl.when(jnp.logical_not(sends))
+        def _():
+            @pl.when(code < 4)
+            def _():
+                own_product(code)
+
+            @pl.when((code >= 8) & (code < 16))
+            def _():
+                other_product(code - 8)
+
+            @pl.when(code == 4)
+            def _():
+                squares()
+
+            @pl.when(code == 5)
+            def _():
+                fragment_sum()
+
+            @pl.when(code == 6)
+            def _():
+                fragment_spread()
+
+            @pl.when(code == 7)
+            def _():
+                fragment_end()
+
+            @pl.when(code == 16 + 16 * CUT)
+            def _():
+                fragment_pass()
+
+            @pl.when((code > 16 + 16 * CUT) & (code <= 16 + 17 * CUT))
+            def _():
+                last_product(code - (17 + 16 * CUT))
+
+            @pl.when(code == 17 + 17 * CUT)
+            def _():
+                row_scale()
+
+    @pl.loop(0, len(words))
     def _(n):
         word = words[0]
         for i in range(1, len(words)):
-            word = jnp.where(n // 4 == i, words[i], word)
-        code = lax.bitwise_and(lax.shift_right_logical(word, 7 * lax.rem(n, 4)), jnp.int32(127))
-
-        @pl.when(code < 4)
-        def _():
-            own_product(code)
-
-        @pl.when((code >= 8) & (code < 16))
-        def _():
-            other_product(code - 8)
-
-        @pl.when((code >= 16) & (code < 16 + 16 * CUT))
-        def _():
-            pass_on(code - 16)
-
-        @pl.when(code == 4)
-        def _():
-            squares()
-
-        @pl.when(code == 5)
-        def _():
-            fragment_sum()
-
-        @pl.when(code == 6)
-        def _():
-            fragment_spread()
-
-        @pl.when(code == 7)
-        def _():
-            fragment_end()
-
-        @pl.when(code == 16 + 16 * CUT)
-        def _():
-            fragment_pass()
+            word = jnp.where(n == i, words[i], word)
+
+        @pl.loop(0, 4)
+        def _(m):
+            do(low(lax.shift_right_logical(word, 7 * m), 128))
 
     for h in range(CUT):
         for s in range(2):
             z_copy(s, h, on_ring(1)).wait_recv()
             z_copy(8 + s, h, on_ring(1)).wait_recv()
 
-            @pl.loop(0, PART // 128)
-            def _(i):
-                rows = pl.ds(pl.multiple_of(i * 128, 128), 128)
-                total = prod[2 * place + s, h, rows, :] + rbuf[s, h, rows, :].astype(F32)
-                total = total + rbuf[8 + s, h, rows, :].astype(F32)
-                out[pl.ds(pl.multiple_of(h * PART + i * 128, 128), 128), s * 128 : (s + 1) * 128] = (total * rsf[h, rows, :]).astype(BF16)
+            total = prod[2 * place + s, h] + rbuf[s, h].astype(F32) + rbuf[8 + s, h].astype(F32)
+            out[h * PART : (h + 1) * PART, s * 128 : (s + 1) * 128] = (total * rsf[h]).astype(BF16)
 
     for copy in x_copies:
         copy.wait_send()
@@ -565,7 +583,7 @@
         scratch_shapes=[
             pltpu.VMEM((TOK, FEAT), BF16),
             pltpu.VMEM((TOK, FEAT), BF16),
-            pltpu.VMEM((1, FEAT), F32),
+            pltpu.VMEM((FEAT,), F32),
             pltpu.VMEM((8, FEAT, 128), BF16),
             pltpu.VMEM((8, FEAT, 128), BF16),
             pltpu.VMEM((16, CUT, PART, 128), F32),
@@ -603,7 +621,7 @@
         compiler_params=pltpu.CompilerParams(
             collective_id=0, has_side_effects=True, vmem_limit_bytes=50 * 1024 * 1024
         ),
-    )(tokens, gain.reshape(1, FEAT), weight, local, base, momentum)
+    )(tokens, pltpu.with_memory_space_constraint(gain, pltpu.HBM), weight, local, base, momentum)
     return pl.pallas_call(
         write_out,
         out_shape=tuple(jax.ShapeDtypeStruct(part.shape, part.dtype) for part in parts),

time: 70.5 us -> 68.9 us (0.977)
  the two profiles are of different devices: /device:TPU:1 before, /device:TPU:30 now
where the time goes in v4:
time: 68.9 us; the launch traced here: 68.8 us
  Pallas kernels  68.1 us (99%)
    pallas_call x1, Pallas kernels, body(): pl.pallas_call(kernel, out_shape=(pltpu.VMEM((TOK, 256), BF16), pltpu.VME...  66.2 us
    pallas_call x1, Pallas kernels, body(): pl.pallas_call(write_out, out_shape=tuple((jax.ShapeDtypeStruct(part.shap...  1.88 us

profile of v4, /device:TPU:30, one launch (start us, length us, event | category | flops | bytes accessed | tf_op | source)
XLA Modules:
  0.0 68.8 jit_solution(17351531818599442208)
XLA Ops:
  0.6 66.2 %shard_map.85 = (bf16[1024,256]{1,0:T(8,128)(2,1)S(1)}, f32[48,8192]{1,0:T(8,128)S(1)}, f32[48,8192]{1,0:T(8,128)S(1)}) custom-call(bf16[1024,1024]{1,0:T(8,128)(2,1)} %tokens.1, f32[1024]{0:T(1024)} %gain.1, bf16[1,1024,1024]{2,1,0:T(8,128)(2,1)} %weight.1, f32[1,48,8192]{2,1,0:T(8,128)} %local.1, f32[48,8192]{1,0:T(8,128)} %base.1, f32[48,8192]{1,0:T(8,128)} %momentum.1), custom_call_target="tpu_custom_call" | custom-call | tf_op jit(solution)/shard_map/pallas_call | solution.py:574
  66.9 1.9 %shard_map.86 = (bf16[1024,256]{1,0:T(8,128)(2,1)}, f32[48,8192]{1,0:T(8,128)}, f32[48,8192]{1,0:T(8,128)}) custom-call(bf16[1024,256]{1,0:T(8,128)(2,1)S(1)} %get-tuple-element.6.a, f32[48,8192]{1,0:T(8,128)S(1)} %get-tuple-element.7.b, f32[48,8192]{1,0:T(8,128)S(1)} %get-tuple-element.8.c), custom_call_target="tpu_custom_call" | custom-call | tf_op jit(solution)/shard_map/pallas_call | solution.py:625

commit v5 on v4

--- a/solution.py
+++ b/solution.py
@@ -28,150 +28,150 @@
 
 ORDER = (
     (
-        0, 8, 1, 3, 64, 65, 2, 66, 4, 9, 67, 76, 40, 41, 77, 42, 78, 43, 68, 10, 85, 69, 32, 33,
-        70, 34, 79, 5, 35, 60, 11, 36, 61, 37, 62, 38, 71, 39, 63, 12, 24, 56, 25, 57, 26, 58, 27, 6,
-        48, 59, 52, 13, 49, 53, 80, 50, 7, 14, 51, 54, 28, 29, 55, 30, 31, 81, 82, 83, 84, 20, 21, 22,
+        2, 8, 0, 1, 3, 64, 65, 4, 9, 66, 67, 40, 41, 76, 42, 77, 43, 78, 10, 79, 36, 37, 85, 68,
+        38, 69, 39, 5, 70, 11, 24, 25, 56, 71, 26, 60, 27, 61, 12, 62, 63, 52, 53, 6, 57, 58, 13, 59,
+        32, 33, 54, 34, 80, 48, 35, 55, 7, 14, 28, 29, 30, 49, 31, 50, 81, 82, 83, 84, 20, 51, 21, 22,
         23, 16, 17, 18, 19,
     ),
     (
-        2, 3, 1, 8, 0, 76, 77, 4, 78, 56, 9, 40, 57, 41, 42, 58, 43, 59, 79, 10, 32, 33, 85, 34,
-        60, 35, 5, 20, 61, 11, 21, 62, 68, 22, 69, 23, 70, 71, 12, 16, 64, 63, 17, 65, 6, 18, 66, 19,
-        67, 48, 13, 36, 49, 37, 38, 50, 80, 39, 51, 52, 7, 14, 28, 29, 53, 54, 30, 55, 31, 81, 82, 83,
+        2, 1, 3, 8, 0, 76, 77, 4, 78, 79, 9, 56, 32, 57, 33, 58, 34, 59, 35, 10, 68, 20, 85, 69,
+        21, 70, 22, 5, 71, 23, 11, 60, 40, 41, 61, 42, 62, 43, 48, 12, 36, 37, 63, 52, 16, 53, 17, 54,
+        6, 18, 55, 19, 38, 13, 64, 65, 39, 66, 80, 67, 49, 7, 14, 28, 29, 50, 51, 30, 31, 81, 82, 83,
         84, 24, 25, 26, 27,
     ),
     (
-        2, 1, 0, 8, 3, 40, 41, 4, 42, 43, 9, 68, 69, 28, 70, 29, 48, 30, 49, 31, 10, 64, 20, 85,
-        65, 21, 66, 22, 5, 67, 23, 11, 50, 24, 51, 36, 71, 25, 52, 26, 12, 76, 27, 77, 37, 78, 38, 6,
-        79, 16, 53, 39, 54, 17, 13, 32, 55, 33, 80, 34, 35, 7, 14, 60, 61, 18, 19, 62, 63, 81, 82, 83,
+        1, 3, 2, 8, 0, 40, 41, 4, 42, 43, 9, 76, 77, 28, 78, 29, 79, 30, 48, 31, 10, 64, 85, 65,
+        20, 66, 21, 5, 67, 22, 11, 68, 23, 69, 24, 70, 25, 71, 26, 12, 52, 27, 36, 53, 37, 54, 38, 49,
+        6, 39, 55, 16, 50, 17, 13, 60, 18, 61, 19, 62, 80, 63, 7, 14, 32, 33, 51, 34, 35, 81, 82, 83,
         84, 56, 57, 58, 59,
     ),
     (
-        3, 1, 0, 8, 2, 36, 37, 4, 38, 76, 77, 39, 9, 78, 28, 79, 29, 30, 31, 10, 32, 64, 65, 85,
-        33, 66, 34, 67, 5, 35, 56, 11, 57, 40, 41, 58, 42, 59, 24, 12, 43, 25, 16, 68, 6, 17, 69, 18,
-        70, 19, 13, 71, 60, 26, 61, 27, 80, 62, 20, 63, 21, 7, 14, 22, 23, 52, 53, 81, 82, 83, 84, 54,
-        55, 48, 49, 50, 51,
-    ),
-    (
-        0, 3, 1, 8, 36, 37, 2, 38, 76, 77, 4, 39, 78, 9, 68, 40, 41, 79, 42, 69, 43, 70, 28, 10,
-        71, 85, 32, 33, 34, 5, 29, 11, 56, 57, 35, 58, 24, 59, 25, 26, 12, 48, 27, 49, 50, 30, 51, 31,
-        20, 13, 16, 64, 65, 17, 66, 18, 67, 19, 60, 14, 21, 61, 22, 62, 23, 63, 81, 82, 83, 84, 52, 53,
-        54, 55, 6, 80, 7,
-    ),
-    (
-        0, 3, 1, 8, 76, 77, 2, 78, 36, 37, 4, 79, 38, 9, 68, 39, 64, 40, 69, 41, 70, 42, 65, 10,
-        28, 85, 71, 43, 66, 32, 67, 33, 5, 34, 11, 60, 61, 35, 62, 29, 63, 30, 48, 31, 12, 49, 24, 50,
-        25, 51, 26, 27, 13, 56, 14, 16, 17, 57, 58, 18, 59, 19, 52, 20, 53, 81, 82, 83, 84, 54, 21, 22,
-        55, 23, 6, 80, 7,
-    ),
-    (
-        2, 1, 3, 8, 76, 77, 0, 78, 40, 41, 4, 79, 42, 9, 43, 68, 69, 36, 70, 32, 71, 33, 60, 10,
-        34, 85, 64, 35, 61, 37, 62, 38, 5, 65, 39, 11, 63, 66, 67, 16, 52, 17, 12, 53, 18, 54, 19, 55,
-        20, 56, 13, 24, 25, 57, 26, 58, 27, 59, 28, 14, 29, 30, 31, 21, 81, 82, 83, 84, 48, 49, 22, 50,
-        51, 6, 23, 80, 7,
-    ),
-    (
-        0, 1, 3, 8, 2, 76, 77, 4, 78, 40, 41, 68, 9, 42, 69, 43, 70, 71, 79, 10, 32, 33, 64, 85,
-        34, 65, 35, 66, 5, 24, 67, 11, 56, 25, 26, 60, 27, 61, 28, 57, 12, 16, 62, 17, 58, 18, 59, 19,
-        63, 13, 36, 52, 37, 53, 38, 54, 39, 48, 14, 49, 29, 30, 50, 20, 51, 21, 55, 81, 82, 83, 84, 22,
-        23, 31, 6, 80, 7,
-    ),
-    (
-        0, 1, 3, 8, 40, 41, 2, 42, 64, 65, 4, 43, 66, 9, 67, 56, 57, 58, 10, 68, 32, 33, 69, 85,
-        34, 70, 35, 48, 5, 49, 11, 36, 37, 50, 38, 51, 39, 71, 59, 12, 28, 29, 60, 30, 31, 24, 13, 76,
-        77, 25, 78, 26, 79, 27, 61, 14, 62, 63, 16, 17, 81, 82, 18, 83, 84, 52, 19, 53, 20, 6, 21, 54,
-        22, 55, 23, 80, 7,
-    ),
-    (
-        2, 1, 0, 8, 3, 76, 77, 4, 78, 79, 9, 40, 41, 56, 42, 57, 43, 58, 16, 59, 10, 48, 20, 85,
-        17, 49, 21, 50, 5, 18, 60, 11, 36, 61, 37, 62, 38, 39, 12, 32, 64, 65, 33, 66, 34, 63, 35, 51,
-        13, 52, 22, 23, 67, 19, 24, 14, 25, 68, 69, 26, 70, 27, 71, 53, 81, 28, 82, 29, 83, 30, 84, 54,
-        55, 31, 6, 80, 7,
-    ),
-    (
-        2, 1, 0, 8, 76, 77, 3, 78, 4, 79, 9, 24, 64, 65, 28, 66, 25, 67, 29, 10, 48, 26, 68, 85,
-        27, 49, 50, 5, 51, 11, 40, 41, 69, 42, 70, 43, 71, 30, 52, 12, 31, 53, 54, 56, 13, 32, 33, 57,
-        58, 34, 55, 35, 14, 36, 37, 59, 38, 39, 20, 81, 60, 82, 61, 83, 62, 84, 21, 22, 63, 23, 6, 16,
-        17, 18, 19, 80, 7,
-    ),
-    (
-        0, 3, 1, 8, 2, 32, 76, 77, 36, 4, 33, 78, 37, 79, 9, 34, 35, 20, 56, 21, 10, 64, 65, 22,
-        85, 66, 23, 67, 38, 5, 57, 39, 11, 68, 69, 70, 16, 71, 12, 40, 41, 58, 59, 42, 43, 17, 13, 18,
-        60, 61, 19, 62, 28, 63, 29, 14, 48, 49, 30, 31, 50, 24, 51, 25, 81, 82, 83, 84, 26, 27, 52, 6,
+        3, 0, 2, 8, 1, 36, 37, 4, 38, 39, 9, 64, 65, 40, 66, 28, 67, 29, 30, 10, 31, 76, 77, 85,
+        32, 78, 33, 79, 5, 34, 11, 35, 68, 69, 41, 70, 42, 71, 43, 12, 24, 56, 57, 25, 58, 26, 59, 27,
+        6, 20, 21, 13, 16, 60, 61, 17, 62, 18, 80, 63, 19, 7, 14, 52, 53, 22, 23, 54, 55, 81, 82, 83,
+        84, 48, 49, 50, 51,
+    ),
+    (
+        2, 0, 3, 8, 1, 36, 37, 76, 77, 4, 38, 39, 78, 9, 40, 79, 41, 42, 43, 10, 64, 65, 32, 85,
+        66, 33, 34, 67, 5, 35, 11, 68, 69, 28, 20, 70, 29, 71, 30, 12, 56, 57, 31, 24, 58, 25, 59, 26,
+        48, 13, 27, 49, 21, 50, 22, 51, 16, 52, 17, 14, 53, 18, 60, 19, 54, 23, 55, 81, 82, 83, 84, 61,
+        62, 63, 6, 80, 7,
+    ),
+    (
+        0, 3, 2, 8, 1, 36, 37, 76, 77, 4, 38, 39, 78, 9, 79, 40, 64, 41, 65, 42, 66, 43, 67, 10,
+        32, 68, 85, 28, 69, 33, 70, 5, 34, 71, 11, 35, 56, 24, 57, 25, 58, 26, 59, 12, 27, 29, 30, 16,
+        48, 13, 49, 20, 21, 50, 22, 51, 31, 23, 14, 60, 61, 17, 62, 18, 63, 19, 81, 82, 83, 84, 52, 6,
         53, 54, 55, 80, 7,
     ),
     (
-        1, 8, 0, 2, 3, 40, 41, 4, 9, 42, 43, 76, 77, 28, 78, 29, 79, 30, 68, 10, 31, 85, 64, 20,
-        65, 21, 66, 5, 22, 67, 11, 23, 69, 16, 70, 24, 71, 17, 12, 56, 57, 18, 19, 58, 25, 59, 6, 26,
-        60, 27, 61, 36, 13, 62, 37, 63, 38, 48, 80, 39, 49, 7, 14, 50, 51, 32, 33, 52, 34, 53, 35, 54,
+        0, 2, 1, 8, 3, 40, 41, 76, 77, 4, 42, 43, 78, 9, 79, 32, 68, 36, 69, 33, 70, 34, 71, 10,
+        24, 64, 85, 35, 65, 25, 66, 5, 26, 67, 11, 27, 56, 37, 57, 38, 58, 28, 59, 12, 29, 60, 30, 61,
+        31, 62, 39, 63, 13, 48, 49, 50, 51, 14, 16, 52, 17, 81, 82, 83, 84, 18, 53, 54, 20, 19, 55, 21,
+        6, 22, 23, 80, 7,
+    ),
+    (
+        3, 0, 2, 8, 1, 76, 77, 40, 41, 4, 78, 79, 42, 9, 43, 68, 32, 64, 33, 69, 34, 70, 35, 10,
+        71, 85, 60, 61, 5, 62, 11, 36, 37, 63, 65, 38, 66, 39, 67, 16, 12, 48, 17, 56, 18, 49, 19, 50,
+        28, 13, 51, 29, 57, 30, 58, 31, 59, 24, 52, 14, 25, 53, 26, 54, 27, 55, 20, 21, 81, 82, 83, 84,
+        22, 23, 6, 80, 7,
+    ),
+    (
+        2, 0, 3, 8, 1, 40, 41, 64, 65, 4, 42, 43, 66, 9, 67, 56, 57, 48, 32, 49, 10, 85, 50, 33,
+        34, 51, 35, 58, 5, 68, 11, 36, 69, 37, 38, 70, 39, 71, 52, 12, 28, 29, 53, 54, 30, 59, 31, 24,
+        13, 25, 76, 77, 26, 78, 27, 79, 14, 55, 16, 60, 17, 61, 81, 82, 18, 83, 84, 62, 19, 63, 20, 6,
+        21, 22, 23, 80, 7,
+    ),
+    (
+        2, 1, 3, 8, 0, 76, 77, 4, 78, 79, 9, 40, 56, 41, 42, 57, 43, 58, 16, 59, 10, 64, 17, 85,
+        20, 65, 18, 66, 5, 19, 67, 11, 36, 48, 37, 49, 38, 50, 39, 60, 12, 32, 61, 33, 62, 34, 63, 35,
+        21, 13, 22, 23, 51, 24, 14, 25, 68, 69, 26, 70, 27, 71, 81, 28, 82, 29, 83, 30, 84, 52, 31, 53,
+        6, 54, 55, 80, 7,
+    ),
+    (
+        1, 0, 2, 8, 3, 76, 77, 4, 78, 79, 9, 64, 24, 65, 25, 66, 28, 67, 26, 10, 48, 27, 85, 49,
+        50, 5, 51, 11, 40, 41, 68, 69, 42, 70, 43, 71, 29, 12, 56, 30, 57, 31, 58, 16, 59, 13, 32, 33,
+        52, 53, 34, 54, 35, 55, 14, 36, 37, 38, 39, 17, 81, 60, 82, 61, 83, 84, 62, 18, 19, 63, 20, 6,
+        21, 22, 23, 80, 7,
+    ),
+    (
+        0, 2, 3, 8, 1, 64, 65, 32, 4, 66, 33, 67, 36, 9, 68, 34, 35, 69, 20, 70, 21, 71, 10, 22,
+        85, 23, 76, 77, 24, 78, 5, 37, 79, 11, 38, 56, 39, 57, 58, 59, 12, 40, 41, 42, 43, 16, 13, 17,
+        60, 61, 18, 62, 19, 63, 25, 14, 48, 49, 26, 27, 50, 28, 51, 29, 81, 82, 83, 84, 30, 31, 52, 6,
+        53, 54, 55, 80, 7,
+    ),
+    (
+        2, 8, 0, 3, 1, 40, 41, 4, 9, 42, 43, 76, 77, 28, 78, 29, 79, 30, 10, 64, 31, 65, 85, 32,
+        66, 20, 67, 5, 21, 11, 56, 57, 22, 23, 58, 16, 59, 17, 68, 12, 18, 69, 19, 70, 24, 71, 25, 6,
+        48, 26, 49, 27, 50, 13, 33, 60, 34, 61, 80, 35, 62, 36, 63, 7, 14, 52, 37, 38, 51, 39, 53, 54,
         81, 82, 83, 84, 55,
     ),
     (
-        2, 0, 3, 8, 1, 64, 65, 36, 37, 4, 66, 38, 67, 9, 39, 76, 28, 77, 29, 68, 30, 69, 31, 10,
-        70, 85, 24, 71, 32, 78, 25, 5, 79, 26, 11, 56, 27, 57, 33, 58, 34, 59, 35, 12, 60, 20, 61, 16,
-        62, 17, 6, 63, 18, 48, 19, 49, 40, 13, 52, 41, 53, 42, 80, 54, 43, 55, 7, 14, 50, 21, 22, 51,
-        81, 82, 83, 84, 23,
-    ),
-    (
-        1, 2, 3, 8, 36, 37, 0, 38, 76, 77, 4, 39, 78, 9, 79, 32, 40, 64, 33, 65, 34, 66, 35, 10,
-        85, 41, 67, 60, 42, 56, 43, 5, 61, 28, 11, 62, 24, 63, 25, 57, 26, 58, 27, 48, 12, 16, 49, 17,
-        50, 18, 51, 6, 19, 52, 29, 53, 30, 13, 54, 20, 55, 21, 59, 80, 22, 68, 7, 14, 23, 31, 69, 70,
+        2, 3, 1, 8, 0, 64, 65, 36, 37, 4, 66, 67, 38, 9, 76, 39, 40, 77, 28, 78, 29, 79, 30, 10,
+        68, 31, 85, 69, 24, 70, 25, 5, 71, 26, 11, 56, 27, 57, 32, 58, 33, 59, 34, 12, 48, 35, 49, 41,
+        50, 42, 51, 6, 43, 60, 61, 13, 62, 20, 21, 63, 22, 80, 23, 52, 7, 14, 53, 54, 55, 81, 82, 83,
+        84, 16, 17, 18, 19,
+    ),
+    (
+        2, 0, 1, 8, 3, 36, 37, 64, 65, 4, 38, 39, 66, 9, 32, 67, 76, 33, 77, 34, 78, 35, 68, 10,
+        85, 69, 40, 41, 70, 42, 71, 5, 43, 79, 11, 24, 60, 25, 61, 26, 62, 27, 63, 12, 28, 56, 29, 57,
+        30, 58, 31, 6, 59, 20, 21, 13, 22, 23, 52, 16, 53, 80, 17, 54, 7, 14, 55, 48, 18, 19, 49, 50,
+        81, 82, 83, 84, 51,
+    ),
+    (
+        3, 0, 2, 8, 40, 41, 1, 42, 64, 65, 4, 43, 66, 9, 36, 56, 37, 57, 38, 58, 39, 59, 32, 10,
+        67, 85, 76, 33, 34, 77, 35, 78, 5, 79, 11, 24, 60, 25, 61, 26, 62, 27, 52, 12, 28, 53, 29, 54,
+        30, 55, 31, 6, 48, 20, 49, 21, 50, 13, 22, 51, 23, 63, 80, 16, 68, 17, 69, 7, 14, 18, 19, 70,
         71, 81, 82, 83, 84,
-    ),
-    (
-        3, 2, 0, 8, 40, 41, 1, 42, 64, 65, 4, 43, 66, 9, 36, 67, 37, 76, 38, 77, 39, 78, 32, 10,
-        56, 85, 57, 33, 34, 58, 35, 59, 5, 79, 11, 24, 52, 25, 68, 26, 53, 27, 54, 12, 28, 55, 29, 69,
-        30, 70, 31, 6, 71, 20, 48, 21, 13, 22, 49, 50, 23, 80, 16, 17, 7, 14, 18, 19, 51, 60, 61, 81,
-        82, 83, 84, 62, 63,
     ),
 )
 ARRIVAL = (
     (
-        9, 8, 10, 11, 12, 13, 15, 14,
-    ),
-    (
-        11, 10, 12, 9, 8, 13, 15, 14,
-    ),
-    (
-        12, 11, 10, 15, 13, 14, 9, 8,
-    ),
-    (
-        15, 10, 12, 14, 13, 11, 9, 8,
-    ),
-    (
-        13, 15, 9, 12, 10, 14, 8, 11,
-    ),
-    (
-        13, 12, 14, 15, 11, 9, 8, 10,
-    ),
-    (
-        10, 15, 9, 13, 11, 8, 12, 14,
-    ),
-    (
-        10, 12, 8, 11, 13, 9, 15, 14,
-    ),
-    (
-        8, 12, 10, 11, 13, 9, 14, 15,
-    ),
-    (
-        11, 10, 12, 13, 8, 14, 9, 15,
+        9, 8, 11, 12, 15, 10, 13, 14,
+    ),
+    (
+        11, 12, 9, 10, 13, 8, 15, 14,
+    ),
+    (
+        12, 13, 10, 11, 15, 9, 14, 8,
+    ),
+    (
+        14, 12, 15, 13, 10, 11, 9, 8,
+    ),
+    (
+        11, 10, 14, 15, 12, 9, 13, 8,
+    ),
+    (
+        13, 10, 14, 12, 8, 9, 15, 11,
+    ),
+    (
+        8, 9, 12, 14, 15, 10, 13, 11,
+    ),
+    (
+        13, 8, 12, 9, 11, 10, 14, 15,
+    ),
+    (
+        8, 10, 12, 11, 13, 9, 14, 15,
+    ),
+    (
+        11, 10, 8, 13, 12, 14, 9, 15,
     ),
     (
         13, 10, 11, 12, 8, 14, 15, 9,
     ),
     (
-        15, 10, 12, 13, 14, 11, 8, 9,
-    ),
-    (
-        15, 13, 14, 9, 12, 10, 11, 8,
-    ),
-    (
-        9, 12, 8, 14, 15, 13, 11, 10,
-    ),
-    (
-        15, 8, 9, 14, 10, 11, 13, 12,
-    ),
-    (
-        9, 8, 10, 11, 13, 12, 15, 14,
+        12, 13, 15, 10, 14, 11, 8, 9,
+    ),
+    (
+        11, 15, 14, 12, 10, 13, 8, 9,
+    ),
+    (
+        13, 14, 10, 15, 12, 9, 11, 8,
+    ),
+    (
+        11, 8, 15, 13, 9, 10, 14, 12,
+    ),
+    (
+        8, 9, 13, 10, 11, 12, 14, 15,
     ),
 )
 

time: 68.9 us -> 69.7 us (1.012)
  the two profiles are of different devices: /device:TPU:30 before, /device:TPU:1 now
where the time goes in v5:
time: 69.7 us; the launch traced here: 69.5 us
  Pallas kernels  68.9 us (99%)
    pallas_call x1, Pallas kernels, body(): pl.pallas_call(kernel, out_shape=(pltpu.VMEM((TOK, 256), BF16), pltpu.VME...  67 us
    pallas_call x1, Pallas kernels, body(): pl.pallas_call(write_out, out_shape=tuple((jax.ShapeDtypeStruct(part.shap...  1.88 us

profile of v5, /device:TPU:1, one launch (start us, length us, event | category | flops | bytes accessed | tf_op | source)
XLA Modules:
  0.0 69.5 jit_solution(9051722684661782586)
XLA Ops:
  0.6 67.0 %shard_map.85 = (bf16[1024,256]{1,0:T(8,128)(2,1)S(1)}, f32[48,8192]{1,0:T(8,128)S(1)}, f32[48,8192]{1,0:T(8,128)S(1)}) custom-call(bf16[1024,1024]{1,0:T(8,128)(2,1)} %tokens.1, f32[1024]{0:T(1024)} %gain.1, bf16[1,1024,1024]{2,1,0:T(8,128)(2,1)} %weight.1, f32[1,48,8192]{2,1,0:T(8,128)} %local.1, f32[48,8192]{1,0:T(8,128)} %base.1, f32[48,8192]{1,0:T(8,128)} %momentum.1), custom_call_target="tpu_custom_call" | custom-call | tf_op jit(solution)/shard_map/pallas_call | solution.py:574
  67.7 1.9 %shard_map.86 = (bf16[1024,256]{1,0:T(8,128)(2,1)}, f32[48,8192]{1,0:T(8,128)}, f32[48,8192]{1,0:T(8,128)}) custom-call(bf16[1024,256]{1,0:T(8,128)(2,1)S(1)} %get-tuple-element.6.a, f32[48,8192]{1,0:T(8,128)S(1)} %get-tuple-element.7.b, f32[48,8192]{1,0:T(8,128)S(1)} %get-tuple-element.8.c), custom_call_target="tpu_custom_call" | custom-call | tf_op jit(solution)/shard_map/pallas_call | solution.py:625
